TPU v7x, 512 devices: a whole 4x4x16 slice. The times are simulated.
512 devices in a mesh: tm: 32 (over z, y_hi), sta: 16 (over x, y_lo, core).
Axes of the slice: x: 4, y: 4 (y_hi: 2, y_lo: 2; y = y_hi * 2 + y_lo), z: 16, core: 2. Of those that a mesh axis runs over, the one named last changes fastest.
Arguments:
- record: float32 [3072, 16384], P('sta', 'tm'), may hold values from -200 to 200
- owner: int32 [96, 1], replicated, may hold values from 0 to 31; in each aligned block of 32 rows (0 to 31, 32 to 63, ...) at most 2 rows name the same one
- offset: int32 [96], replicated, may hold values from 0 to 511
- station: int32 [3072], P('sta'), may hold values from 0 to 1023, as said below
- valid: int32 [3072], P('sta'), may hold values 0 or 1
Outputs:
- stack: float32 [3, 32, 16384], P(None, 'sta', 'tm')
Inputs may be any that keep to these rules, and one draw needn't show every extreme that they name: `owner`: among the 32 templates of one step (rows i * 32 to i * 32 + 31) no time block is named more than 2 times, and some block is named exactly 2 times in some step. Every station number names exactly 3 channels.
All inputs are finite; a program needn't handle non-finite values. No bound on the sum of `valid` on one device may be relied on, other than what follows from the above.
Results may differ from a plain program's by a relative error of at most 0.0015.
Values may be sent and summed in bfloat16 or wider, within the bound.
No kernel may reach another device: no remote copies, remote signals or barrier semaphores. Data moves between devices by JAX's collectives and lax.ppermute only.
A program may use at most 64 MiB of HBM per device.

v0:
```python
import math

import jax
import jax.numpy as jnp
from jax import lax
from jax.sharding import PartitionSpec as P

WIN = 100
TPL_STEP = 32
NSTEP = 3


EPSILON = 1e-05


def shifted(array, axis, by):
    length = lax.axis_size(axis)
    pairs = [(i, i + by) for i in range(length) if 0 <= i + by < length]
    return lax.ppermute(array, axis, pairs)


def normalize(pieces):
    values = pieces.astype(jnp.float32)
    centred = values - jnp.mean(values, axis=-1, keepdims=True)
    spread = jnp.sqrt(jnp.mean(centred * centred, axis=-1, keepdims=True) + EPSILON)
    return (centred / (WIN * spread)).astype(jnp.bfloat16)


def body(record, owner, offset, station, valid):
    ch_dev, samp_dev = record.shape
    rounded = record.astype(jnp.bfloat16)
    edge_cells = shifted(rounded[:, : WIN - 1], "tm", -1)
    extended = jnp.concatenate([rounded, edge_cells], axis=1)
    stations = ch_dev * lax.axis_size("sta") // 3
    station_table = (station[:, None] == jnp.arange(stations, dtype=jnp.int32)[None, :]).astype(
        jnp.float32
    )
    present = valid.astype(jnp.float32)
    local_counts = jnp.dot(present, station_table, precision=lax.Precision.HIGHEST)
    counts = lax.psum(local_counts, "sta")
    own_counts = jnp.dot(station_table, counts, precision=lax.Precision.HIGHEST)
    weight = present / jnp.maximum(own_counts, 1.0)
    position = lax.axis_index("tm")
    row_len = ch_dev * WIN

    def template_at(first_sample):
        return normalize(lax.dynamic_slice_in_dim(extended, first_sample, WIN, 1)).reshape(row_len)

    def fetch_step(step_number):
        first_row = step_number * TPL_STEP
        own_step = owner[first_row : first_row + TPL_STEP, 0]
        off_step = offset[first_row : first_row + TPL_STEP]
        capacity = max(2, 2 * TPL_STEP // lax.axis_size("tm"))
        template_index = jnp.arange(TPL_STEP, dtype=jnp.int32)
        earlier = (own_step[None, :] == own_step[:, None]) & (
            template_index[None, :] < template_index[:, None]
        )
        slot_rank = jnp.sum(earlier.astype(jnp.int32), axis=1)
        owned_here = own_step == position
        slot_pick = owned_here[None, :] & (
            slot_rank[None, :] == jnp.arange(capacity, dtype=jnp.int32)[:, None]
        )
        slot_start = jnp.sum(jnp.where(slot_pick, off_step[None, :], 0), axis=1)
        filled = jnp.any(slot_pick, axis=1)
        slot_rows = jax.vmap(template_at)(slot_start)
        slot_rows = jnp.where(filled[:, None], slot_rows, jnp.zeros_like(slot_rows))
        everyone = lax.all_gather(slot_rows, "tm", axis=0, tiled=True)
        return jnp.take(everyone, own_step * capacity + slot_rank, axis=0)

    block_size = 8
    block_count = ch_dev // block_size
    factor = 1.0 / math.sqrt(stations)
    fetched = jnp.concatenate([fetch_step(step_number) for step_number in range(NSTEP)], axis=0)
    row_count = fetched.shape[0]
    shaped = fetched.reshape(row_count, block_count, block_size * WIN)

    def add_block(running, block_index):
        channel_rows = lax.dynamic_slice_in_dim(extended, block_index * block_size, block_size, 0)
        hankel = jnp.stack([channel_rows[:, k : k + samp_dev] for k in range(WIN)], axis=1)
        values = hankel.astype(jnp.float32)
        window_mean = jnp.mean(values, axis=1)
        window_square = jnp.mean(values * values, axis=1)
        inverse = 1.0 / jnp.sqrt(
            jnp.maximum(window_square - window_mean * window_mean, 0.0) + EPSILON
        )
        scaled = lax.dynamic_slice_in_dim(weight, block_index * block_size, block_size, 0)
        window = (values * (scaled[:, None] * inverse)[:, None, :]).astype(jnp.bfloat16)
        template_part = lax.dynamic_index_in_dim(shaped, block_index, 1, keepdims=False)
        product = jnp.dot(
            template_part,
            window.reshape(block_size * WIN, samp_dev),
            preferred_element_type=jnp.float32,
        )
        return (running + product, None)

    running, unused = lax.scan(
        add_block,
        jnp.zeros((row_count, samp_dev), jnp.float32),
        jnp.arange(block_count, dtype=jnp.int32),
    )
    partial_stack = running.reshape(NSTEP, TPL_STEP, samp_dev)
    summed = lax.psum_scatter(partial_stack, "sta", scatter_dimension=1, tiled=True)
    return summed * factor


def solution(mesh):
    placed = (P("sta", "tm"), P(), P(), P("sta"), P("sta"))
    return jax.shard_map(
        body, mesh=mesh, in_specs=placed, out_specs=P(None, "sta", "tm"), check_vma=False
    )
```

profile of v0, /device:TPU:1, one launch (start us, length us, event | category | flops | bytes accessed | tf_op | source)
XLA Modules:
  0.0 991.3 jit_solution(10041407845333885053)
XLA Ops:
  7.6 1.3 collective-permute-start
  14.3 33.4 %psum.7 = f32[1024]{0:T(1024)S(1)} all-reduce(f32[1024]{0:T(1024)S(1)} %bitcast.676), channel_id=1, replica_groups=mesh['tm'=32,'sta'=16] {'sta'}, use_global_device_ids=true, to_apply=%region_0.0 | all-reduce | flops 1024 | bytes 8192 | tf_op jit(solution)/shard_map/psum | solution.py:40
  50.2 2.5 while.15
  54.5 2.8 while.14
  57.7 2.7 while.16
  63.6 135.3 %all-gather.9.cloned.1.call-done = bf16[32,2,19200]{2,1,0:T(2,128)(2,1)} async-done(((bf16[1,2,19200]{2,1,0:T(2,128)(2,1)}), bf16[32,2,19200]{2,1,0:T(2,128)(2,1)}) %all-gather.9.cloned.1.call-update) | async-done | bytes 2457616 | tf_op jit(solution)/shard_map/all_gather | solution.py:67
  198.9 2.9 reshape.269
  201.8 2.4 gather_fusion.1
  204.2 2.5 broadcast_select_fusion.1
  206.7 142.3 %all-gather.7.cloned.1.call-done = bf16[32,2,19200]{2,1,0:T(2,128)(2,1)} async-done(((bf16[1,2,19200]{2,1,0:T(2,128)(2,1)}), bf16[32,2,19200]{2,1,0:T(2,128)(2,1)}) %all-gather.7.cloned.1.call-update) | async-done | bytes 2457616 | tf_op jit(solution)/shard_map/all_gather | solution.py:67
  349.1 2.9 reshape.267
  352.0 2.4 gather_fusion
  354.4 2.5 broadcast_select_fusion.2
  356.9 142.3 %all-gather.11.cloned.1.call-done = bf16[32,2,19200]{2,1,0:T(2,128)(2,1)} async-done(((bf16[1,2,19200]{2,1,0:T(2,128)(2,1)}), bf16[32,2,19200]{2,1,0:T(2,128)(2,1)}) %all-gather.11.cloned.1.call-update) | async-done | bytes 2457616 | tf_op jit(solution)/shard_map/all_gather | solution.py:67
  499.3 2.9 reshape.271
  502.2 2.4 gather_fusion.2
  504.6 1.6 broadcast_select_fusion
  506.6 1.9 pad_maximum_fusion
  508.5 9.3 reshape.180
  517.8 4.6 copy.23
  522.4 329.6 %while.17 = (s32[]{:T(128)}, f32[96,512]{1,0:T(8,128)S(1)}, s32[24]{0:T(128)S(1)}, bf16[96,24,800]{2,0,1:T(8,128)(2,1)}, bf16[192,611]{1,0:T(8,128)(2,1)S(1)}, /...) while((s32[]{:T(128)}, f32[96,512]{1,0:T(8,128)S(1)}, ...), condition=%wide.region_19.21_spmd.clone, body=%wide.region_16.20_spmd.clone.sunk | while | flops 81629296 | bytes 8858643 | solution.py:96
  534.9 1.2 convolution_add_fusion.2
  548.6 1.2 convolution_add_fusion.2
  562.4 1.2 convolution_add_fusion.2
  576.1 1.2 convolution_add_fusion.2
  589.9 1.2 convolution_add_fusion.2
  603.6 1.2 convolution_add_fusion.2
  617.3 1.2 convolution_add_fusion.2
  631.1 1.2 convolution_add_fusion.2
  644.8 1.2 convolution_add_fusion.2
  658.5 1.2 convolution_add_fusion.2
  672.3 1.2 convolution_add_fusion.2
  686.0 1.2 convolution_add_fusion.2
  699.7 1.2 convolution_add_fusion.2
  713.5 1.2 convolution_add_fusion.2
  727.2 1.2 convolution_add_fusion.2
  740.9 1.2 convolution_add_fusion.2
  754.7 1.2 convolution_add_fusion.2
  768.4 1.2 convolution_add_fusion.2
  782.1 1.2 convolution_add_fusion.2
  795.9 1.2 convolution_add_fusion.2
  809.6 1.2 convolution_add_fusion.2
  823.3 1.2 convolution_add_fusion.2
  837.1 1.2 convolution_add_fusion.2
  850.8 1.2 convolution_add_fusion.2
  852.8 1.3 dynamic-slice.12
  854.7 128.6 %all-reduce.6.cloned.1.call-done = f32[3,32,512]{2,1,0:T(8,128)} async-done(((f32[3,32,512]{2,1,0:T(8,128)}), f32[3,32,512]{2,1,0:T(8,128)}) %all-reduce.6.cloned.1.call-update) | async-done | bytes 196624
  983.3 1.4 dynamic-slice_multiply_fusion
  (2657 shorter events, 260.2 us)
Async XLA Ops:
  6.5 192.4 %all-gather.9.cloned.1.call-start = ((), (), s32[]{:S(2)}) async-start(), calls=%async_computation.1 | async-start | bytes 2534400 | tf_op jit(solution)/shard_map/all_gather | solution.py:67
  7.6 42.5 %collective-permute-start = (bf16[192,99]{1,0:T(8,128)(2,1)S(1)}, bf16[192,99]{1,0:T(8,128)(2,1)S(1)}, u32[]{:S(2)}, u32[]{:S(2)}) collective-permute-start(bf16[192,99]{1,0:T(8,128)(2,1)S(1)} %slice.467), channel_id=1, source_target_pairs={{16,0},{32,16},{48,32},{64,48},{80,64},{96,80},{112,96},{128,112},... | collective-permute-start | bytes 114056 | tf_op jit(solution)/shard_map/ppermute | solution.py:19
  54.4 294.7 %all-gather.7.cloned.1.call-start = ((), (), s32[]{:S(2)}) async-start(), calls=%async_computation | async-start | bytes 2534400 | tf_op jit(solution)/shard_map/all_gather | solution.py:67
  61.8 437.5 %all-gather.11.cloned.1.call-start = ((), (), s32[]{:S(2)}) async-start(), calls=%async_computation.2 | async-start | bytes 2534400 | tf_op jit(solution)/shard_map/all_gather | solution.py:67
  63.4 920.0 %all-reduce.6.cloned.1.call-start = ((), (), s32[]{:S(2)}) async-start(), calls=%async_computation.3 | async-start | bytes 393216
  504.6 1.7 copy-start.1
  504.6 2.0 copy-start.2
  852.1 0.7 copy-start
Sparse Core Ops, SparseCore 0:
  54.5 144.3 all-gather.8
  202.0 147.0 all-gather.6
  352.2 147.0 all-gather.10
  852.9 130.3 all-reduce.5
where the time goes:
time: 993 us; the launch traced here: 991 us
  waiting for transfers between devices  549 us (55%)
  local copies, waits for them, and re-layouts  269 us (27%)
  loops' own time  63.1 us (6%)
  blocking collectives  33.4 us (3%)
  matrix products  31.9 us (3%)
  other arithmetic  29.8 us (3%)
  between operations  14 us (1%)
    all_gather x3, waiting for transfers between devices, fetch_step(): everyone = lax.all_gather(slot_rows, 'tm', axis=0, tiled=True)  420 us
    while x2376, local copies, waits for them, and re-layouts  197 us
    unnamed x5, waiting for transfers between devices  129 us
    another operation x1, loops' own time, body(): lax.scan(add_block, jnp.zeros((row_count, samp_dev), jnp.float32), jnp.ar...  62.9 us
    psum x1, blocking collectives, body(): counts = lax.psum(local_counts, 'sta')  33.4 us
    dot_general x24, matrix products, add_block(): jnp.dot(template_part, window.reshape(block_size * WIN, samp_dev), prefer...  29.6 us
  transfers between devices with their start and end apart: 5, of which 4 were waited for; matrix products, arithmetic and copies ran while one was open for 3% of the time, Pallas kernels for 0%

commit v1 on v0

v1 whole, which is shorter than its diff:
```python
import functools

import jax
import jax.numpy as jnp
from jax import lax
from jax.experimental import pallas as pl
from jax.experimental.pallas import tpu as pltpu
from jax.sharding import Mesh
from jax.sharding import PartitionSpec as P

WIN = 100
EPSILON = 1e-05
NTPL = 96
NSTEP = 3
TPL_STEP = 32
BLOCK = 512
LANES = 128
BASE = 16
GROUPS = 7

FAR = ("zh",)
NEAR = ("zl", "yh")
TM = FAR + NEAR
STA = ("x", "yl", "core")


def shift_left(value, by):
    if by == 0:
        return value
    return pltpu.roll(value, value.shape[1] - by, axis=1)


def correlate(
    group_ref, start_ref, rec_ref, codes_ref, own_ref, out_ref,
    tiles, ext, raw, tmat, base32, base16, scale, win, acc,
):
    blocks, chans, _ = rec_ref.shape
    n_near = ext.shape[1] // BLOCK
    samples = n_near * BLOCK
    wide = samples + LANES
    group = group_ref[0]
    per_block = BLOCK // LANES

    def copy_block(b, carry):
        values = rec_ref[b].astype(jnp.float32)
        for q in range(per_block):
            tiles[b * per_block + q] = values[:, q * LANES : (q + 1) * LANES]
        return carry

    lax.fori_loop(0, blocks, copy_block, 0)
    tiles[blocks * per_block] = jnp.zeros((chans, LANES), jnp.float32)

    first_tile = group * (n_near * per_block)
    for q in range(n_near * per_block + 1):
        ext[:, q * LANES : (q + 1) * LANES] = tiles[first_tile + q]

    def take_template(row, carry):
        start = start_ref[row]
        tile = start // LANES
        rest = start - tile * LANES
        back = lax.rem(LANES - rest, LANES)
        low = pltpu.roll(tiles[tile], back, axis=1)
        high = pltpu.roll(tiles[tile + 1], back, axis=1)
        lane = lax.broadcasted_iota(jnp.int32, (chans, LANES), 1)
        raw[pl.ds(row, chans, stride=NTPL), :] = jnp.where(lane < LANES - rest, low, high)
        return carry

    lax.fori_loop(0, NTPL, take_template, 0, unroll=8)

    lane = lax.broadcasted_iota(jnp.int32, (NTPL, LANES), 1)
    inside = lane < WIN
    for c in range(chans):
        values = jnp.where(inside, raw[c * NTPL : (c + 1) * NTPL, :], 0.0)
        mean = jnp.sum(values, axis=1, keepdims=True) / WIN
        centred = jnp.where(inside, values - mean, 0.0)
        spread = jnp.sqrt(jnp.sum(centred * centred, axis=1, keepdims=True) / WIN + EPSILON)
        tmat[:, c * LANES : (c + 1) * LANES] = (centred / (WIN * spread)).astype(jnp.bfloat16)

    codes = codes_ref[...].astype(jnp.int32)
    own = own_ref[...].astype(jnp.int32)
    own_station = own // 2
    own_valid = own - own_station * 2
    counts = jnp.zeros((chans, LANES), jnp.int32)
    for r in range(codes.shape[0]):
        row = codes[r : r + 1, :]
        station = row // 2
        counts = counts + jnp.where(own_station == station, row - station * 2, 0)
    total = jnp.sum(counts.astype(jnp.float32), axis=1, keepdims=True)
    weight = own_valid.astype(jnp.float32) / jnp.maximum(total, 1.0)

    values = ext[...]

    def window_sum(v):
        two = v + shift_left(v, 1)
        four = two + shift_left(two, 2)
        eight = four + shift_left(four, 4)
        sixteen = eight + shift_left(eight, 8)
        most = sixteen + shift_left(sixteen, 16)
        most64 = most + shift_left(most, 32)
        return most64 + shift_left(most, 64) + shift_left(four, 96)

    mean = window_sum(values) / WIN
    square = window_sum(values * values) / WIN
    inverse = 1.0 / jnp.sqrt(jnp.maximum(square - mean * mean, 0.0) + EPSILON)
    scale[...] = (weight * inverse)[:, :samples]

    for q in range(n_near * per_block + 1):
        low = tiles[first_tile + q]
        high = tiles[jnp.minimum(first_tile + q + 1, blocks * per_block)]
        pair = jnp.concatenate([low, high], axis=1)
        for i in range(BASE):
            base32[pl.ds(i, chans, stride=BASE), :] = shift_left(pair, i)[:, :LANES]
        base16[q] = base32[...].astype(jnp.bfloat16)

    for c in range(chans):
        win[c * LANES + GROUPS * BASE : (c + 1) * LANES, :] = jnp.zeros(
            (LANES - GROUPS * BASE, BLOCK), jnp.bfloat16
        )

    def one_block(e, carry):
        first = pl.multiple_of(e * BLOCK, BLOCK)

        def one_channel(c, inner):
            rows = pl.ds(pl.multiple_of(c * BASE, BASE), BASE)
            piece = jnp.concatenate(
                [base16[e * per_block + q, rows, :] for q in range(per_block + 1)], axis=1
            )
            factor = scale[pl.ds(c, 1), pl.ds(first, BLOCK)]
            for g in range(GROUPS):
                moved = shift_left(piece, g * BASE)[:, :BLOCK]
                win[pl.ds(pl.multiple_of(c * LANES + g * BASE, BASE), BASE), :] = (
                    moved.astype(jnp.float32) * factor
                ).astype(jnp.bfloat16)
            return inner

        lax.fori_loop(0, chans, one_channel, 0, unroll=2)
        product = jnp.dot(tmat[...], win[...], preferred_element_type=jnp.float32)
        n_sta = out_ref.shape[0]
        per_sta = NTPL // n_sta
        for r in range(per_sta):
            for q in range(per_block):
                acc[q, pl.ds(e * per_sta + r, n_sta, stride=n_near * per_sta), :] = product[
                    r * n_sta : (r + 1) * n_sta, q * LANES : (q + 1) * LANES
                ]
        return carry

    lax.fori_loop(0, n_near, one_block, 0)
    rows = n_near * NTPL // out_ref.shape[0]
    for j in range(out_ref.shape[0]):
        for q in range(per_block):
            out_ref[j, :, q * LANES : (q + 1) * LANES] = acc[q, j * rows : (j + 1) * rows, :].astype(
                jnp.bfloat16
            )


def body(record, owner, offset, station, valid):
    ch_dev, samp_dev = record.shape
    n_far, n_near, n_sta = lax.axis_size(FAR), lax.axis_size(NEAR), lax.axis_size(STA)
    chans = ch_dev // n_near
    per_sta = NTPL // n_sta

    code = (station * 2 + valid).astype(jnp.float32)
    codes = lax.all_to_all(
        jnp.broadcast_to(code[None, :], (n_sta, ch_dev)), STA, 0, 0, tiled=True
    ).reshape(n_sta * ch_dev // LANES, LANES)
    own = lax.dynamic_slice_in_dim(code, lax.axis_index(NEAR) * chans, chans)[:, None]

    rounded = record.astype(jnp.bfloat16).reshape(n_near, chans, samp_dev)
    mine = lax.all_to_all(rounded, NEAR, 0, 0, tiled=True)
    whole = lax.all_gather(mine, FAR, axis=0, tiled=True)

    starts = owner[:, 0] * samp_dev + offset
    starts = starts.reshape(NSTEP, n_sta, per_sta // NSTEP).transpose(0, 2, 1).reshape(NTPL)
    group = lax.axis_index(FAR).astype(jnp.int32).reshape(1)

    samples = n_near * samp_dev
    wide = samples + LANES
    smem = pl.BlockSpec(memory_space=pltpu.SMEM)
    vmem = pl.BlockSpec(memory_space=pltpu.VMEM)
    f32, bf16 = jnp.float32, jnp.bfloat16
    part = pl.pallas_call(
        correlate,
        out_shape=jax.ShapeDtypeStruct((n_sta, n_near * per_sta, samp_dev), bf16),
        in_specs=[smem, smem, vmem, vmem, vmem],
        out_specs=vmem,
        scratch_shapes=[
            pltpu.VMEM((n_far * n_near * samp_dev // LANES + 1, chans, LANES), f32),
            pltpu.VMEM((chans, wide), f32),
            pltpu.VMEM((chans * NTPL, LANES), f32),
            pltpu.VMEM((NTPL, chans * LANES), bf16),
            pltpu.VMEM((chans * BASE, LANES), f32),
            pltpu.VMEM((wide // LANES, chans * BASE, LANES), bf16),
            pltpu.VMEM((chans, samples), f32),
            pltpu.VMEM((chans * LANES, samp_dev), bf16),
            pltpu.VMEM((samp_dev // LANES, n_near * NTPL, LANES), f32),
        ],
        compiler_params=pltpu.CompilerParams(vmem_limit_bytes=48 * 1024 * 1024),
        cost_estimate=pl.CostEstimate(
            flops=2 * NTPL * chans * LANES * samples, bytes_accessed=2 << 20, transcendentals=0
        ),
    )(group, starts, whole, codes, own)

    moved = lax.all_to_all(part, STA, 0, 0, tiled=True)
    summed = jnp.sum(moved.astype(f32), axis=0).reshape(n_near, per_sta, samp_dev)
    last = lax.all_to_all(summed, NEAR, 0, 0, tiled=True)
    result = jnp.sum(last, axis=0) * (1.0 / 32.0)
    return result.reshape(NSTEP, per_sta // NSTEP, samp_dev)


def solution(mesh):
    fine = Mesh(mesh.devices.reshape(4, 4, 2, 4, 2, 2), TM + STA)
    placed = (P(STA, TM), P(), P(), P(STA), P(STA))
    return jax.shard_map(
        body, mesh=fine, in_specs=placed, out_specs=P(None, STA, TM), check_vma=False
    )
```

time: 993 us -> 128 us (0.13)
  waiting for transfers between devices: 549 us -> 11.9 us
  local copies, waits for them, and re-layouts: 269 us -> 1.77 us
  loops' own time: 63.1 us -> 0 us
  blocking collectives: 33.4 us -> 66.8 us
  matrix products: 31.9 us -> 0 us
  Pallas kernels: 0 us -> 29.5 us
  other arithmetic: 29.8 us -> 2.6 us
  between operations: 14 us -> 0.06 us
  starting transfers between devices: 1.6 us -> 14.7 us
    all_gather x3 -> x0, waiting for transfers between devices: 420 us -> none  [fetch_step(): everyone = lax.all_gather(slot_rows, 'tm', axis=0, tiled=True)]
    while x2376 -> x0, local copies, waits for them, and re-layouts: 197 us -> none
    unnamed x5 -> x0, waiting for transfers between devices: 129 us -> none
    another operation x4 -> x0, loops' own time: 63.1 us -> none  [the longest x1 62.9 us: body(): lax.scan(add_block, jnp.zeros((row_count, samp_dev), jnp.float32), jnp.ar...]
    all_gather x0 -> x1, blocking collectives: none -> 35.5 us  [body(): whole = lax.all_gather(mine, FAR, axis=0, tiled=True)]
    psum x1 -> x0, blocking collectives: 33.4 us -> none  [body(): counts = lax.psum(local_counts, 'sta')]
    dot_general x26 -> x0, matrix products: 31.9 us -> none  [the longest x24 29.6 us: add_block(): jnp.dot(template_part, window.reshape(block_size * WIN, samp_dev), prefer...]
    all_to_all x0 -> x2, blocking collectives: none -> 31.3 us  [the longest x1 20.3 us: body(): moved = lax.all_to_all(part, STA, 0, 0, tiled=True)]
  transfers between devices with their start and end apart: 5 -> 2, of which waited for: 4 -> 2; matrix products, arithmetic and copies ran while one was open for 3% -> 2% of each run, Pallas kernels for 0% -> 0%
where the time goes in v1:
time: 128 us; the launch traced here: 127 us
  blocking collectives  66.8 us (52%)
  Pallas kernels  29.5 us (23%)
  starting transfers between devices  14.7 us (11%)
  waiting for transfers between devices  11.9 us (9%)
  other arithmetic  2.6 us (2%)
  local copies, waits for them, and re-layouts  1.77 us (1%)
    all_gather x1, blocking collectives, body(): whole = lax.all_gather(mine, FAR, axis=0, tiled=True)  35.5 us
    pallas_call x1, Pallas kernels, body(): pl.pallas_call(correlate, out_shape=jax.ShapeDtypeStruct((n_sta, n_near *...  29.5 us
    all_to_all x1, blocking collectives, body(): moved = lax.all_to_all(part, STA, 0, 0, tiled=True)  20.3 us
    all_to_all x1, blocking collectives, body(): last = lax.all_to_all(summed, NEAR, 0, 0, tiled=True)  11 us
    all_to_all x1, starting transfers between devices, body(): lax.all_to_all(jnp.broadcast_to(code[None, :], (n_sta, ch_dev)), STA, 0,...  10.1 us
    all_to_all x1, waiting for transfers between devices, body(): mine = lax.all_to_all(rounded, NEAR, 0, 0, tiled=True)  7.75 us
    all_to_all x1, starting transfers between devices, body(): mine = lax.all_to_all(rounded, NEAR, 0, 0, tiled=True)  4.59 us
    all_to_all x1, waiting for transfers between devices, body(): lax.all_to_all(jnp.broadcast_to(code[None, :], (n_sta, ch_dev)), STA, 0,...  4.16 us
  transfers between devices with their start and end apart: 2, of which 2 were waited for; matrix products, arithmetic and copies ran while one was open for 2% of the time, Pallas kernels for 0%

profile of v1, /device:TPU:1, one launch (start us, length us, event | category | flops | bytes accessed | tf_op | source)
XLA Modules:
  0.0 127.4 jit_solution(14726999864512285432)
XLA Ops:
  0.0 0.0 copy-start
  0.0 0.0 copy-start.1
  0.0 0.7 add_convert_fusion
  0.7 0.6 broadcast_in_dim.4
  1.3 10.1 %all-to-all-start.1 = ((f32[16,1,192]{2,1,0:T(1,128)}), f32[16,1,192]{2,1,0:T(1,128)S(1)}, u32[]{:S(2)}, u32[]{:S(2)}) async-start(f32[16,1,192]{2,1,0:T(1,128)} %broadcast_in_dim.4), calls=%async_computation.1 | async-start | bytes 32768 | tf_op jit(solution)/shard_map/all_to_all | solution.py:163
  11.5 1.7 %convert_element_type.9 = bf16[192,512]{1,0:T(8,128)(2,1)} convert(f32[192,512]{1,0:T(8,128)} %param.5) | non-fusion elementwise | flops 98304 | bytes 589824 | tf_op jit(solution)/shard_map/convert_element_type | solution.py:168
  13.2 4.2 %all-to-all-done.1 = f32[16,1,192]{2,1,0:T(1,128)S(1)} async-done(((f32[16,1,192]{2,1,0:T(1,128)}), f32[16,1,192]{2,1,0:T(1,128)S(1)}, u32[]{:S(2)}, u32[]{:S(2)}) %all-to-all-start.1) | async-done | bytes 12320 | tf_op jit(solution)/shard_map/all_to_all | solution.py:163
  17.3 4.6 %all-to-all-start = ((bf16[8,24,512]{2,1,0:T(8,128)(2,1)}), bf16[8,24,512]{2,1,0:T(8,128)(2,1)S(1)}, u32[]{:S(2)}, u32[]{:S(2)}) async-start(bf16[8,24,512]{2,1,0:T(8,128)(2,1)} %bitcast.3), calls=%async_computation | async-start | bytes 393216 | tf_op jit(solution)/shard_map/all_to_all | solution.py:169
  21.9 0.1 dynamic-slice_bitcast_fusion
  22.0 0.1 copy.11.own_ref
  22.1 0.0 copy-done
  22.1 0.0 copy-done.1
  22.1 0.1 reshape.32
  22.2 0.1 copy.10
  22.3 0.1 reshape.33.start_ref
  22.4 0.1 reduce
  22.5 0.1 reshape.35.codes_ref
  22.5 7.7 %all-to-all-done = bf16[8,24,512]{2,1,0:T(8,128)(2,1)S(1)} async-done(((bf16[8,24,512]{2,1,0:T(8,128)(2,1)}), bf16[8,24,512]{2,1,0:T(8,128)(2,1)S(1)}, u32[]{:S(2)}, u32[]{:S(2)}) %all-to-all-start) | async-done | bytes 196640 | tf_op jit(solution)/shard_map/all_to_all | solution.py:169
  30.3 35.5 %all_gather.3.rec_ref = bf16[32,24,512]{2,1,0:T(8,128)(2,1)S(1)} all-gather(bf16[8,24,512]{2,1,0:T(8,128)(2,1)S(1)} %all-to-all-done), channel_id=1, replica_groups=mesh['zh'=4,'zl'=4,'yh'=2,'x'=4,'yl'=2,'core'=2] {'zh'}, dimensions={0}, use_global_device_ids=true | all-gather | bytes 983040 | tf_op jit(solution)/shard_map/all_gather | solution.py:170
  65.8 29.5 %shard_map.55 = bf16[16,48,512]{2,1,0:T(8,128)(2,1)S(1)} custom-call(s32[1]{0:T(128)} %bitcast.group_ref, s32[96]{0:T(128)S(1)} %reshape.33.start_ref, bf16[32,24,512]{2,1,0:T(8,128)(2,1)S(1)} %all_gather.3.rec_ref, f32[24,128]{1,0:T(8,128)S(1)} %reshape.35.codes_ref, f32[24,1]{1,0:T(8,128)S(1)} %copy.11.own_ref), custom_call_target="tpu_custom_call" | custom-call | flops 2415919104 | bytes 2097152 | tf_op jit(solution)/shard_map/pallas_call | solution.py:181
  95.3 20.3 %all_to_all.21 = bf16[16,48,512]{2,1,0:T(8,128)(2,1)S(1)} all-to-all(bf16[16,48,512]{2,1,0:T(8,128)(2,1)S(1)} %shard_map.55), channel_id=1, replica_groups=mesh['zh'=4,'zl'=4,'yh'=2,'x'=4,'yl'=2,'core'=2] {'x','yl','core'}, dimensions={0} | all-to-all | bytes 1572864 | tf_op jit(solution)/shard_map/all_to_all | solution.py:203
  115.6 0.1 convert_reduce_fusion
  115.8 11.0 %all_to_all.22 = f32[8,6,512]{2,1,0:T(8,128)S(1)} all-to-all(f32[8,6,512]{2,1,0:T(8,128)S(1)} %reshape.36), channel_id=1, replica_groups=mesh['zh'=4,'zl'=4,'yh'=2,'x'=4,'yl'=2,'core'=2] {'zl','yh'}, dimensions={0} | all-to-all | bytes 196608 | tf_op jit(solution)/shard_map/all_to_all | solution.py:205
  126.8 0.6 mul.40
  (4 shorter events, 0.0 us)
Async XLA Ops:
  0.0 22.1 %copy-start = (s32[96]{0:T(128)S(1)}, s32[96]{0:T(128)}, u32[]{:S(2)}) copy-start(s32[96]{0:T(128)} %param.7) | copy-start | bytes 1156
  0.0 22.1 %copy-start.1 = (s32[96,1]{0,1:T(1,128)S(1)}, s32[96,1]{0,1:T(1,128)}, u32[]{:S(2)}) copy-start(s32[96,1]{0,1:T(1,128)} %param.6) | copy-start | bytes 1156
  1.3 16.0 %all-to-all-start.1 = ((f32[16,1,192]{2,1,0:T(1,128)}), f32[16,1,192]{2,1,0:T(1,128)S(1)}, u32[]{:S(2)}, u32[]{:S(2)}) async-start(f32[16,1,192]{2,1,0:T(1,128)} %broadcast_in_dim.4), calls=%async_computation.1 | async-start | bytes 32768 | tf_op jit(solution)/shard_map/all_to_all | solution.py:163
  17.3 12.9 %all-to-all-start = ((bf16[8,24,512]{2,1,0:T(8,128)(2,1)}), bf16[8,24,512]{2,1,0:T(8,128)(2,1)S(1)}, u32[]{:S(2)}, u32[]{:S(2)}) async-start(bf16[8,24,512]{2,1,0:T(8,128)(2,1)} %bitcast.3), calls=%async_computation | async-start | bytes 393216 | tf_op jit(solution)/shard_map/all_to_all | solution.py:169

commit v2 on v1

v2 whole, which is shorter than its diff:
```python
import jax
import jax.numpy as jnp
from jax import lax
from jax.experimental import pallas as pl
from jax.experimental.pallas import tpu as pltpu
from jax.sharding import Mesh
from jax.sharding import PartitionSpec as P

WIN = 100
EPSILON = 1e-05
NTPL = 96
NSTEP = 3
TPL_STEP = 32
BLOCK = 512
LANES = 128
PER_BLOCK = BLOCK // LANES
BASE = 16
GROUPS = 7

RUN = 8
TM = ("zh", "zl", "yh")
SPLIT = ("zl", "yh")
GATHER = "zh"
STA = ("x", "yl", "core")

SMEM = pl.BlockSpec(memory_space=pltpu.SMEM)
VMEM = pl.BlockSpec(memory_space=pltpu.VMEM)
F32, BF16 = jnp.float32, jnp.bfloat16


def shift_left(value, by):
    if by == 0:
        return value
    return pltpu.roll(value, value.shape[1] - by, axis=1)


def deviations(values):
    def window_sum(v):
        two = v + shift_left(v, 1)
        four = two + shift_left(two, 2)
        eight = four + shift_left(four, 4)
        sixteen = eight + shift_left(eight, 8)
        half = sixteen + shift_left(sixteen, 16)
        whole = half + shift_left(half, 32)
        return whole + shift_left(half, 64) + shift_left(four, 96)

    mean = window_sum(values) / WIN
    square = window_sum(values * values) / WIN
    return 1.0 / jnp.sqrt(jnp.maximum(square - mean * mean, 0.0) + EPSILON)


def shifted_base(tile, n_tiles, base32, base16):
    chans = tile(0).shape[0]
    lane = lax.broadcasted_iota(jnp.int32, (chans, LANES), 1)
    low = [shift_left(tile(0), i) for i in range(BASE)]
    for q in range(n_tiles):
        if q < n_tiles - 1:
            high = [shift_left(tile(q + 1), i) for i in range(BASE)]
        else:
            high = [jnp.zeros((chans, LANES), F32)] * BASE
        for i in range(BASE):
            base32[pl.ds(i, chans, stride=BASE), :] = jnp.where(lane < LANES - i, low[i], high[i])
        base16[q] = base32[...].astype(BF16)
        low = high


def fill_windows(base16, first, count, factor, store):
    chans = base16.shape[1] // BASE
    for c in range(chans):
        piece = jnp.concatenate(
            [base16[first + q, c * BASE : (c + 1) * BASE, :] for q in range(count + 1)], axis=1
        )
        for g in range(GROUPS):
            moved = shift_left(piece, g * BASE)[:, : count * LANES]
            store(c * LANES + g * BASE, (moved.astype(F32) * factor(c)).astype(BF16))


def stack_kernel(
    group_ref, start_ref, rec_ref, codes_ref, own_ref, out_ref,
    tiles, ext, raw, tmat, base32, base16, scale, win0, win1, acc,
):
    n_gather, n_split, chans, _ = rec_ref.shape
    n_sta = out_ref.shape[0]
    per_sta = NTPL // n_sta
    n_runs = n_split // RUN
    run_tiles = RUN * PER_BLOCK + 1

    for l in range(n_gather):
        for h in range(n_runs):
            for y in range(RUN):
                block = (h * n_gather + l) * RUN + y
                for q in range(PER_BLOCK):
                    tiles[block * PER_BLOCK + q] = rec_ref[
                        l, h * RUN + y, :, q * LANES : (q + 1) * LANES
                    ].astype(F32)
    tiles[n_gather * n_split * PER_BLOCK] = jnp.zeros((chans, LANES), F32)

    for h in range(n_runs):
        first = (h * n_gather + group_ref[0]) * (RUN * PER_BLOCK)
        for q in range(run_tiles):
            place = (h * run_tiles + q) * LANES
            ext[:, place : place + LANES] = tiles[first + q]
    scale[...] = deviations(ext[...])
    shifted_base(
        lambda q: ext[:, q * LANES : (q + 1) * LANES], n_runs * run_tiles, base32, base16
    )

    def take_template(row, carry):
        start = start_ref[row]
        tile = start // LANES
        rest = start - tile * LANES
        back = lax.rem(LANES - rest, LANES)
        low = pltpu.roll(tiles[tile], back, axis=1)
        high = pltpu.roll(tiles[tile + 1], back, axis=1)
        lane = lax.broadcasted_iota(jnp.int32, (chans, LANES), 1)
        raw[pl.ds(row, chans, stride=NTPL), :] = jnp.where(lane < LANES - rest, low, high)
        return carry

    lax.fori_loop(0, NTPL, take_template, 0, unroll=16)

    codes = codes_ref[...].astype(jnp.int32)
    own = own_ref[...].astype(jnp.int32)
    own_station = own // 2
    own_valid = own - own_station * 2
    counts = jnp.zeros((chans, codes.shape[1]), jnp.int32)
    for r in range(codes.shape[0]):
        row = codes[r : r + 1, :]
        station = row // 2
        counts = counts + jnp.where(own_station == station, row - station * 2, 0)
    total = jnp.sum(counts.astype(F32), axis=1, keepdims=True)
    weight = own_valid.astype(F32) / jnp.maximum(total, 1.0)

    lane = lax.broadcasted_iota(jnp.int32, (NTPL, LANES), 1)
    inside = lane < WIN
    for c in range(chans):
        values = jnp.where(inside, raw[c * NTPL : (c + 1) * NTPL, :], 0.0)
        mean = jnp.sum(values, axis=1, keepdims=True) / WIN
        centred = jnp.where(inside, values - mean, 0.0)
        spread = jnp.sqrt(jnp.sum(centred * centred, axis=1, keepdims=True) / WIN + EPSILON)
        scaled = centred * (weight[c : c + 1, :] / (WIN * spread))
        tmat[:, c * LANES : (c + 1) * LANES] = scaled.astype(BF16)

    spare = jnp.zeros((LANES - GROUPS * BASE, BLOCK), BF16)
    for win in (win0, win1):
        for c in range(chans):
            win[c * LANES + GROUPS * BASE : (c + 1) * LANES, :] = spare

    def fill(e, win):
        first = e // RUN * run_tiles + e % RUN * PER_BLOCK
        lanes = pl.ds(pl.multiple_of(first * LANES, LANES), BLOCK)

        def store(row, values):
            win[row : row + BASE, :] = values

        fill_windows(base16, first, PER_BLOCK, lambda c: scale[c : c + 1, lanes], store)

    def multiply(e, win):
        product = jnp.dot(tmat[...], win[...], preferred_element_type=F32)
        for r in range(per_sta):
            for q in range(PER_BLOCK):
                acc[q, pl.ds(e * per_sta + r, n_sta, stride=n_split * per_sta), :] = product[
                    r * n_sta : (r + 1) * n_sta, q * LANES : (q + 1) * LANES
                ]

    fill(0, win0)

    def two_blocks(i, carry):
        multiply(2 * i, win0)
        fill(2 * i + 1, win1)
        multiply(2 * i + 1, win1)
        fill(2 * i + 2, win0)
        return carry

    lax.fori_loop(0, n_split // 2 - 1, two_blocks, 0)
    multiply(n_split - 2, win0)
    fill(n_split - 1, win1)
    multiply(n_split - 1, win1)
    rows = n_split * per_sta
    for j in range(n_sta):
        for q in range(PER_BLOCK):
            out_ref[j, :, q * LANES : (q + 1) * LANES] = acc[
                q, j * rows : (j + 1) * rows, :
            ].astype(BF16)


def body(record, owner, offset, station, valid):
    ch_dev, samp_dev = record.shape
    n_gather, n_split, n_sta = lax.axis_size(GATHER), lax.axis_size(SPLIT), lax.axis_size(STA)
    chans = ch_dev // n_split
    per_sta = NTPL // n_sta
    runs = n_split // RUN
    wide = runs * (RUN * PER_BLOCK + 1) * LANES

    code = (station * 2 + valid).astype(F32)
    codes = lax.all_to_all(
        jnp.broadcast_to(code[None, :], (n_sta, ch_dev)), STA, 0, 0, tiled=True
    ).reshape(n_sta * ch_dev // LANES, LANES)
    own = lax.dynamic_slice_in_dim(code, lax.axis_index(SPLIT) * chans, chans)[:, None]

    rounded = record.astype(BF16).reshape(n_split, chans, samp_dev)
    mine = lax.all_to_all(rounded, SPLIT, 0, 0, tiled=True)
    whole = lax.all_gather(mine, GATHER, axis=0, tiled=False)

    starts = owner[:, 0] * samp_dev + offset
    starts = starts.reshape(NSTEP, n_sta, per_sta // NSTEP).transpose(0, 2, 1).reshape(NTPL)
    group = lax.axis_index(GATHER).astype(jnp.int32).reshape(1)

    part = pl.pallas_call(
        stack_kernel,
        out_shape=jax.ShapeDtypeStruct((n_sta, n_split * per_sta, samp_dev), BF16),
        in_specs=[SMEM, SMEM, VMEM, VMEM, VMEM],
        out_specs=VMEM,
        scratch_shapes=[
            pltpu.VMEM((n_gather * n_split * PER_BLOCK + 1, chans, LANES), F32),
            pltpu.VMEM((chans, wide), F32),
            pltpu.VMEM((chans * NTPL, LANES), F32),
            pltpu.VMEM((NTPL, chans * LANES), BF16),
            pltpu.VMEM((chans * BASE, LANES), F32),
            pltpu.VMEM((wide // LANES, chans * BASE, LANES), BF16),
            pltpu.VMEM((chans, wide), F32),
            pltpu.VMEM((chans * LANES, samp_dev), BF16),
            pltpu.VMEM((chans * LANES, samp_dev), BF16),
            pltpu.VMEM((PER_BLOCK, n_split * NTPL, LANES), F32),
        ],
        compiler_params=pltpu.CompilerParams(vmem_limit_bytes=48 * 1024 * 1024),
        cost_estimate=pl.CostEstimate(
            flops=14_000_000_000, bytes_accessed=2 << 20, transcendentals=0
        ),
    )(group, starts, whole, codes, own)

    moved = lax.all_to_all(part, STA, 0, 0, tiled=True)
    summed = jnp.sum(moved.astype(F32), axis=0).reshape(n_split, per_sta, samp_dev)
    final = lax.all_to_all(summed, SPLIT, 0, 0, tiled=True)
    result = jnp.sum(final, axis=0) * (1.0 / 32.0)
    return result.reshape(NSTEP, per_sta // NSTEP, samp_dev)


def solution(mesh):
    fine = Mesh(mesh.devices.reshape(4, 4, 2, 4, 2, 2), TM + STA)
    placed = (P(STA, TM), P(), P(), P(STA), P(STA))
    return jax.shard_map(
        body, mesh=fine, in_specs=placed, out_specs=P(None, STA, TM), check_vma=False
    )
```

time: 128 us -> 116 us (0.906)
  Pallas kernels: 29.5 us -> 17.4 us
    pallas_call x1, Pallas kernels: 29.5 us -> 17.4 us  [body(): pl.pallas_call(stack_kernel, out_shape=jax.ShapeDtypeStruct((n_sta, n_spl...]
where the time goes in v2:
time: 116 us; the launch traced here: 115 us
  blocking collectives  66.8 us (58%)
  Pallas kernels  17.4 us (15%)
  starting transfers between devices  14.7 us (13%)
  waiting for transfers between devices  11.9 us (10%)
  other arithmetic  2.6 us (2%)
  local copies, waits for them, and re-layouts  1.77 us (2%)
    all_gather x1, blocking collectives, body(): whole = lax.all_gather(mine, GATHER, axis=0, tiled=False)  35.5 us
    all_to_all x1, blocking collectives, body(): moved = lax.all_to_all(part, STA, 0, 0, tiled=True)  20.3 us
    pallas_call x1, Pallas kernels, body(): pl.pallas_call(stack_kernel, out_shape=jax.ShapeDtypeStruct((n_sta, n_spl...  17.4 us
    all_to_all x1, blocking collectives, body(): final = lax.all_to_all(summed, SPLIT, 0, 0, tiled=True)  11 us
    all_to_all x1, starting transfers between devices, body(): lax.all_to_all(jnp.broadcast_to(code[None, :], (n_sta, ch_dev)), STA, 0,...  10.1 us
    all_to_all x1, waiting for transfers between devices, body(): mine = lax.all_to_all(rounded, SPLIT, 0, 0, tiled=True)  7.75 us
    all_to_all x1, starting transfers between devices, body(): mine = lax.all_to_all(rounded, SPLIT, 0, 0, tiled=True)  4.59 us
    all_to_all x1, waiting for transfers between devices, body(): lax.all_to_all(jnp.broadcast_to(code[None, :], (n_sta, ch_dev)), STA, 0,...  4.16 us
  transfers between devices with their start and end apart: 2, of which 2 were waited for; matrix products, arithmetic and copies ran while one was open for 2% of the time, Pallas kernels for 0%

profile of v2, /device:TPU:1, one launch (start us, length us, event | category | flops | bytes accessed | tf_op | source)
XLA Modules:
  0.0 115.3 jit_solution(10822354971364674528)
XLA Ops:
  0.0 0.0 copy-start
  0.0 0.0 copy-start.1
  0.0 0.7 add_convert_fusion
  0.7 0.6 broadcast_in_dim.4
  1.3 10.1 %all-to-all-start.1 = ((f32[16,1,192]{2,1,0:T(1,128)}), f32[16,1,192]{2,1,0:T(1,128)S(1)}, u32[]{:S(2)}, u32[]{:S(2)}) async-start(f32[16,1,192]{2,1,0:T(1,128)} %broadcast_in_dim.4), calls=%async_computation.1 | async-start | bytes 32768 | tf_op jit(solution)/shard_map/all_to_all | solution.py:195
  11.5 1.7 %convert_element_type.9 = bf16[192,512]{1,0:T(8,128)(2,1)} convert(f32[192,512]{1,0:T(8,128)} %param.5) | non-fusion elementwise | flops 98304 | bytes 589824 | tf_op jit(solution)/shard_map/convert_element_type | solution.py:200
  13.2 4.2 %all-to-all-done.1 = f32[16,1,192]{2,1,0:T(1,128)S(1)} async-done(((f32[16,1,192]{2,1,0:T(1,128)}), f32[16,1,192]{2,1,0:T(1,128)S(1)}, u32[]{:S(2)}, u32[]{:S(2)}) %all-to-all-start.1) | async-done | bytes 12320 | tf_op jit(solution)/shard_map/all_to_all | solution.py:195
  17.3 4.6 %all-to-all-start = ((bf16[8,24,512]{2,1,0:T(8,128)(2,1)}), bf16[8,24,512]{2,1,0:T(8,128)(2,1)S(1)}, u32[]{:S(2)}, u32[]{:S(2)}) async-start(bf16[8,24,512]{2,1,0:T(8,128)(2,1)} %bitcast.3), calls=%async_computation | async-start | bytes 393216 | tf_op jit(solution)/shard_map/all_to_all | solution.py:201
  21.9 0.1 dynamic-slice_bitcast_fusion
  22.0 0.1 copy.11.own_ref
  22.1 0.0 copy-done
  22.1 0.0 copy-done.1
  22.1 0.1 reshape.32
  22.2 0.1 copy.10
  22.3 0.1 reshape.33.start_ref
  22.4 0.1 reduce
  22.5 0.1 reshape.35.codes_ref
  22.5 7.7 %all-to-all-done = bf16[8,24,512]{2,1,0:T(8,128)(2,1)S(1)} async-done(((bf16[8,24,512]{2,1,0:T(8,128)(2,1)}), bf16[8,24,512]{2,1,0:T(8,128)(2,1)S(1)}, u32[]{:S(2)}, u32[]{:S(2)}) %all-to-all-start) | async-done | bytes 196640 | tf_op jit(solution)/shard_map/all_to_all | solution.py:201
  30.3 35.5 %all-gather = bf16[32,24,512]{2,1,0:T(8,128)(2,1)S(1)} all-gather(bf16[8,24,512]{2,1,0:T(8,128)(2,1)S(1)} %all-to-all-done), channel_id=2, replica_groups=mesh['zh'=4,'zl'=4,'yh'=2,'x'=4,'yl'=2,'core'=2] {'zh'}, dimensions={0}, use_global_device_ids=true | all-gather | bytes 983040 | tf_op jit(solution)/shard_map/all_gather | solution.py:202
  65.8 17.4 %shard_map.55 = bf16[16,48,512]{2,1,0:T(8,128)(2,1)S(1)} custom-call(s32[1]{0:T(128)} %bitcast.group_ref, s32[96]{0:T(128)S(1)} %reshape.33.start_ref, bf16[4,8,24,512]{3,2,1,0:T(8,128)(2,1)S(1)} %bitcast.8, f32[24,128]{1,0:T(8,128)S(1)} %reshape.35.codes_ref, f32[24,1]{1,0:T(8,128)S(1)} %copy.11.own_ref), custom_call_target="tpu_custom_call" | custom-call | flops 14000000000 | bytes 2097152 | tf_op jit(solution)/shard_map/pallas_call | solution.py:208
  83.2 20.3 %all_to_all.21 = bf16[16,48,512]{2,1,0:T(8,128)(2,1)S(1)} all-to-all(bf16[16,48,512]{2,1,0:T(8,128)(2,1)S(1)} %shard_map.55), channel_id=1, replica_groups=mesh['zh'=4,'zl'=4,'yh'=2,'x'=4,'yl'=2,'core'=2] {'x','yl','core'}, dimensions={0} | all-to-all | bytes 1572864 | tf_op jit(solution)/shard_map/all_to_all | solution.py:231
  103.5 0.1 convert_reduce_fusion
  103.7 11.0 %all_to_all.22 = f32[8,6,512]{2,1,0:T(8,128)S(1)} all-to-all(f32[8,6,512]{2,1,0:T(8,128)S(1)} %reshape.36), channel_id=1, replica_groups=mesh['zh'=4,'zl'=4,'yh'=2,'x'=4,'yl'=2,'core'=2] {'zl','yh'}, dimensions={0} | all-to-all | bytes 196608 | tf_op jit(solution)/shard_map/all_to_all | solution.py:233
  114.7 0.6 mul.40
  (4 shorter events, 0.0 us)
Async XLA Ops:
  0.0 22.1 %copy-start = (s32[96]{0:T(128)S(1)}, s32[96]{0:T(128)}, u32[]{:S(2)}) copy-start(s32[96]{0:T(128)} %param.7) | copy-start | bytes 1156
  0.0 22.1 %copy-start.1 = (s32[96,1]{0,1:T(1,128)S(1)}, s32[96,1]{0,1:T(1,128)}, u32[]{:S(2)}) copy-start(s32[96,1]{0,1:T(1,128)} %param.6) | copy-start | bytes 1156
  1.3 16.0 %all-to-all-start.1 = ((f32[16,1,192]{2,1,0:T(1,128)}), f32[16,1,192]{2,1,0:T(1,128)S(1)}, u32[]{:S(2)}, u32[]{:S(2)}) async-start(f32[16,1,192]{2,1,0:T(1,128)} %broadcast_in_dim.4), calls=%async_computation.1 | async-start | bytes 32768 | tf_op jit(solution)/shard_map/all_to_all | solution.py:195
  17.3 12.9 %all-to-all-start = ((bf16[8,24,512]{2,1,0:T(8,128)(2,1)}), bf16[8,24,512]{2,1,0:T(8,128)(2,1)S(1)}, u32[]{:S(2)}, u32[]{:S(2)}) async-start(bf16[8,24,512]{2,1,0:T(8,128)(2,1)} %bitcast.3), calls=%async_computation | async-start | bytes 393216 | tf_op jit(solution)/shard_map/all_to_all | solution.py:201

commit v3 on v2

--- a/solution.py
+++ b/solution.py
@@ -34,22 +34,34 @@
     return pltpu.roll(value, value.shape[1] - by, axis=1)
 
 
+def dot(left, right):
+    return jnp.dot(left.astype(BF16), right, preferred_element_type=F32)
+
+
+def two_parts(value):
+    high = value.astype(BF16)
+    return high, value - high.astype(F32)
+
+
 def deviations(values):
-    def window_sum(v):
-        two = v + shift_left(v, 1)
-        four = two + shift_left(two, 2)
-        eight = four + shift_left(four, 4)
-        sixteen = eight + shift_left(eight, 8)
-        half = sixteen + shift_left(sixteen, 16)
-        whole = half + shift_left(half, 32)
-        return whole + shift_left(half, 64) + shift_left(four, 96)
-
-    mean = window_sum(values) / WIN
-    square = window_sum(values * values) / WIN
+    n_tiles, chans, _ = values.shape
+    flat = values.reshape(n_tiles * chans, LANES)
+    row = lax.broadcasted_iota(jnp.int32, (LANES, LANES), 0)
+    lane = lax.broadcasted_iota(jnp.int32, (LANES, LANES), 1)
+    own = ((row >= lane) & (row < lane + WIN)).astype(F32).astype(BF16)
+    after = (row + LANES < lane + WIN).astype(F32).astype(BF16)
+
+    def window_sum(parts):
+        here = sum(dot(part, own) for part in parts).reshape(n_tiles, chans, LANES)
+        there = sum(dot(part, after) for part in parts).reshape(n_tiles, chans, LANES)
+        return here[:-1] + there[1:]
+
+    mean = window_sum([flat]) / WIN
+    square = window_sum(two_parts(flat * flat)) / WIN
     return 1.0 / jnp.sqrt(jnp.maximum(square - mean * mean, 0.0) + EPSILON)
 
 
-def shifted_base(tile, n_tiles, base32, base16):
+def shifted_base(tile, n_tiles, base32, base16, place):
     chans = tile(0).shape[0]
     lane = lax.broadcasted_iota(jnp.int32, (chans, LANES), 1)
     low = [shift_left(tile(0), i) for i in range(BASE)]
@@ -60,7 +72,7 @@
             high = [jnp.zeros((chans, LANES), F32)] * BASE
         for i in range(BASE):
             base32[pl.ds(i, chans, stride=BASE), :] = jnp.where(lane < LANES - i, low[i], high[i])
-        base16[q] = base32[...].astype(BF16)
+        base16[place + q] = base32[...].astype(BF16)
         low = high
 
 
@@ -77,7 +89,7 @@
 
 def stack_kernel(
     group_ref, start_ref, rec_ref, codes_ref, own_ref, out_ref,
-    tiles, ext, raw, tmat, base32, base16, scale, win0, win1, acc,
+    tiles, raw, tmat, base32, base16, scale, win0, win1, acc,
 ):
     n_gather, n_split, chans, _ = rec_ref.shape
     n_sta = out_ref.shape[0]
@@ -94,29 +106,6 @@
                         l, h * RUN + y, :, q * LANES : (q + 1) * LANES
                     ].astype(F32)
     tiles[n_gather * n_split * PER_BLOCK] = jnp.zeros((chans, LANES), F32)
-
-    for h in range(n_runs):
-        first = (h * n_gather + group_ref[0]) * (RUN * PER_BLOCK)
-        for q in range(run_tiles):
-            place = (h * run_tiles + q) * LANES
-            ext[:, place : place + LANES] = tiles[first + q]
-    scale[...] = deviations(ext[...])
-    shifted_base(
-        lambda q: ext[:, q * LANES : (q + 1) * LANES], n_runs * run_tiles, base32, base16
-    )
-
-    def take_template(row, carry):
-        start = start_ref[row]
-        tile = start // LANES
-        rest = start - tile * LANES
-        back = lax.rem(LANES - rest, LANES)
-        low = pltpu.roll(tiles[tile], back, axis=1)
-        high = pltpu.roll(tiles[tile + 1], back, axis=1)
-        lane = lax.broadcasted_iota(jnp.int32, (chans, LANES), 1)
-        raw[pl.ds(row, chans, stride=NTPL), :] = jnp.where(lane < LANES - rest, low, high)
-        return carry
-
-    lax.fori_loop(0, NTPL, take_template, 0, unroll=16)
 
     codes = codes_ref[...].astype(jnp.int32)
     own = own_ref[...].astype(jnp.int32)
@@ -130,15 +119,35 @@
     total = jnp.sum(counts.astype(F32), axis=1, keepdims=True)
     weight = own_valid.astype(F32) / jnp.maximum(total, 1.0)
 
+    for h in range(n_runs):
+        first = (h * n_gather + group_ref[0]) * (RUN * PER_BLOCK)
+        values = tiles[pl.ds(first, run_tiles)]
+        scale[h * run_tiles : (h + 1) * run_tiles - 1] = weight[None] * deviations(values)
+        shifted_base(lambda q: tiles[first + q], run_tiles, base32, base16, h * run_tiles)
+
+    def take_template(row, carry):
+        start = start_ref[row]
+        tile = start // LANES
+        rest = start - tile * LANES
+        back = lax.rem(LANES - rest, LANES)
+        low = pltpu.roll(tiles[tile], back, axis=1)
+        high = pltpu.roll(tiles[tile + 1], back, axis=1)
+        lane = lax.broadcasted_iota(jnp.int32, (chans, LANES), 1)
+        raw[pl.ds(row, chans, stride=NTPL), :] = jnp.where(lane < LANES - rest, low, high)
+        return carry
+
+    lax.fori_loop(0, NTPL, take_template, 0, unroll=96)
+
     lane = lax.broadcasted_iota(jnp.int32, (NTPL, LANES), 1)
     inside = lane < WIN
+    ones = jnp.ones((LANES, LANES), BF16)
     for c in range(chans):
         values = jnp.where(inside, raw[c * NTPL : (c + 1) * NTPL, :], 0.0)
-        mean = jnp.sum(values, axis=1, keepdims=True) / WIN
+        mean = dot(values, ones) / WIN
         centred = jnp.where(inside, values - mean, 0.0)
-        spread = jnp.sqrt(jnp.sum(centred * centred, axis=1, keepdims=True) / WIN + EPSILON)
-        scaled = centred * (weight[c : c + 1, :] / (WIN * spread))
-        tmat[:, c * LANES : (c + 1) * LANES] = scaled.astype(BF16)
+        total = sum(dot(part, ones) for part in two_parts(centred * centred))
+        spread = jnp.sqrt(total / WIN + EPSILON)
+        tmat[:, c * LANES : (c + 1) * LANES] = (centred / (WIN * spread)).astype(BF16)
 
     spare = jnp.zeros((LANES - GROUPS * BASE, BLOCK), BF16)
     for win in (win0, win1):
@@ -147,12 +156,14 @@
 
     def fill(e, win):
         first = e // RUN * run_tiles + e % RUN * PER_BLOCK
-        lanes = pl.ds(pl.multiple_of(first * LANES, LANES), BLOCK)
 
         def store(row, values):
             win[row : row + BASE, :] = values
 
-        fill_windows(base16, first, PER_BLOCK, lambda c: scale[c : c + 1, lanes], store)
+        def factor(c):
+            return jnp.concatenate([scale[first + q, c : c + 1, :] for q in range(PER_BLOCK)], axis=1)
+
+        fill_windows(base16, first, PER_BLOCK, factor, store)
 
     def multiply(e, win):
         product = jnp.dot(tmat[...], win[...], preferred_element_type=F32)
@@ -192,13 +203,14 @@
     wide = runs * (RUN * PER_BLOCK + 1) * LANES
 
     code = (station * 2 + valid).astype(F32)
+
+    rounded = record.astype(BF16).reshape(n_split, chans, samp_dev)
+    mine = lax.all_to_all(rounded, SPLIT, 0, 0, tiled=True)
+    mine, code = lax.optimization_barrier((mine, code))
     codes = lax.all_to_all(
         jnp.broadcast_to(code[None, :], (n_sta, ch_dev)), STA, 0, 0, tiled=True
     ).reshape(n_sta * ch_dev // LANES, LANES)
     own = lax.dynamic_slice_in_dim(code, lax.axis_index(SPLIT) * chans, chans)[:, None]
-
-    rounded = record.astype(BF16).reshape(n_split, chans, samp_dev)
-    mine = lax.all_to_all(rounded, SPLIT, 0, 0, tiled=True)
     whole = lax.all_gather(mine, GATHER, axis=0, tiled=False)
 
     starts = owner[:, 0] * samp_dev + offset
@@ -212,12 +224,11 @@
         out_specs=VMEM,
         scratch_shapes=[
             pltpu.VMEM((n_gather * n_split * PER_BLOCK + 1, chans, LANES), F32),
-            pltpu.VMEM((chans, wide), F32),
             pltpu.VMEM((chans * NTPL, LANES), F32),
             pltpu.VMEM((NTPL, chans * LANES), BF16),
             pltpu.VMEM((chans * BASE, LANES), F32),
             pltpu.VMEM((wide // LANES, chans * BASE, LANES), BF16),
-            pltpu.VMEM((chans, wide), F32),
+            pltpu.VMEM((wide // LANES, chans, LANES), F32),
             pltpu.VMEM((chans * LANES, samp_dev), BF16),
             pltpu.VMEM((chans * LANES, samp_dev), BF16),
             pltpu.VMEM((PER_BLOCK, n_split * NTPL, LANES), F32),

time: 116 us -> 112 us (0.966)
  waiting for transfers between devices: 11.9 us -> 7.82 us
  Pallas kernels: 17.4 us -> 14.4 us
  blocking collectives: 66.8 us -> 69.7 us
    all_to_all x1, starting transfers between devices: 4.59 us -> 9.08 us  [body(): mine = lax.all_to_all(rounded, SPLIT, 0, 0, tiled=True)]
    all_to_all x1, waiting for transfers between devices: 4.16 us -> 0.01 us  [body(): lax.all_to_all(jnp.broadcast_to(code[None, :], (n_sta, ch_dev)), STA, 0,...]
    all_to_all x1, starting transfers between devices: 10.1 us -> 6.67 us  [body(): lax.all_to_all(jnp.broadcast_to(code[None, :], (n_sta, ch_dev)), STA, 0,...]
    pallas_call x1, Pallas kernels: 17.4 us -> 14.4 us  [body(): pl.pallas_call(stack_kernel, out_shape=jax.ShapeDtypeStruct((n_sta, n_spl...]
    all_gather x1, blocking collectives: 35.5 us -> 37.8 us  [body(): whole = lax.all_gather(mine, GATHER, axis=0, tiled=False)]
    all_to_all x1, blocking collectives: 11 us -> 12.7 us  [body(): final = lax.all_to_all(summed, SPLIT, 0, 0, tiled=True)]
  transfers between devices with their start and end apart: 2 -> 2, of which waited for: 2 -> 1; matrix products, arithmetic and copies ran while one was open for 2% -> 0% of each run, Pallas kernels for 0% -> 0%
where the time goes in v3:
time: 112 us; the launch traced here: 111 us
  blocking collectives  69.7 us (62%)
  starting transfers between devices  15.8 us (14%)
  Pallas kernels  14.4 us (13%)
  waiting for transfers between devices  7.82 us (7%)
  other arithmetic  1.92 us (2%)
  local copies, waits for them, and re-layouts  1.77 us (2%)
    all_gather x1, blocking collectives, body(): whole = lax.all_gather(mine, GATHER, axis=0, tiled=False)  37.8 us
    all_to_all x1, blocking collectives, body(): moved = lax.all_to_all(part, STA, 0, 0, tiled=True)  19.3 us
    pallas_call x1, Pallas kernels, body(): pl.pallas_call(stack_kernel, out_shape=jax.ShapeDtypeStruct((n_sta, n_spl...  14.4 us
    all_to_all x1, blocking collectives, body(): final = lax.all_to_all(summed, SPLIT, 0, 0, tiled=True)  12.7 us
    all_to_all x1, starting transfers between devices, body(): mine = lax.all_to_all(rounded, SPLIT, 0, 0, tiled=True)  9.08 us
    all_to_all x1, waiting for transfers between devices, body(): mine = lax.all_to_all(rounded, SPLIT, 0, 0, tiled=True)  7.82 us
    all_to_all x1, starting transfers between devices, body(): lax.all_to_all(jnp.broadcast_to(code[None, :], (n_sta, ch_dev)), STA, 0,...  6.67 us
  transfers between devices with their start and end apart: 2, of which 1 were waited for; matrix products, arithmetic and copies ran while one was open for 0% of the time, Pallas kernels for 0%

profile of v3, /device:TPU:1, one launch (start us, length us, event | category | flops | bytes accessed | tf_op | source)
XLA Modules:
  0.0 111.5 jit_solution(308886176864588126)
XLA Ops:
  0.0 0.0 copy-start.2
  0.0 0.0 copy-start.3
  0.0 0.0 copy-start
  0.0 0.0 copy-start.1
  0.0 1.7 %convert_element_type.9 = bf16[192,512]{1,0:T(8,128)(2,1)} convert(f32[192,512]{1,0:T(8,128)} %param.5) | non-fusion elementwise | flops 98304 | bytes 589824 | tf_op jit(solution)/shard_map/convert_element_type | solution.py:207
  1.8 9.1 %all-to-all-start = ((bf16[8,24,512]{2,1,0:T(8,128)(2,1)}), bf16[8,24,512]{2,1,0:T(8,128)(2,1)S(1)}, u32[]{:S(2)}, u32[]{:S(2)}) async-start(bf16[8,24,512]{2,1,0:T(8,128)(2,1)} %bitcast.3), calls=%async_computation | async-start | bytes 393216 | tf_op jit(solution)/shard_map/all_to_all | solution.py:208
  10.8 0.0 copy-done.2
  10.8 0.0 copy-done.3
  10.9 0.1 reshape.32
  11.0 0.1 copy.10
  11.1 0.1 reshape.33.start_ref
  11.2 0.0 copy-done
  11.2 0.0 copy-done.1
  11.2 7.8 %all-to-all-done = bf16[8,24,512]{2,1,0:T(8,128)(2,1)S(1)} async-done(((bf16[8,24,512]{2,1,0:T(8,128)(2,1)}), bf16[8,24,512]{2,1,0:T(8,128)(2,1)S(1)}, u32[]{:S(2)}, u32[]{:S(2)}) %all-to-all-start) | async-done | bytes 196640 | tf_op jit(solution)/shard_map/all_to_all | solution.py:208
  19.0 0.6 broadcast_in_dim.4
  19.6 6.7 %all-to-all-start.1 = ((f32[16,1,192]{2,1,0:T(1,128)}), f32[16,1,192]{2,1,0:T(1,128)S(1)}, u32[]{:S(2)}, u32[]{:S(2)}) async-start(f32[16,1,192]{2,1,0:T(1,128)} %broadcast_in_dim.4), calls=%async_computation.1 | async-start | bytes 32768 | tf_op jit(solution)/shard_map/all_to_all | solution.py:210
  26.3 37.8 %all-gather = bf16[32,24,512]{2,1,0:T(8,128)(2,1)S(1)} all-gather(bf16[8,24,512]{2,1,0:T(8,128)(2,1)S(1)} %all-to-all-done), channel_id=2, replica_groups=mesh['zh'=4,'zl'=4,'yh'=2,'x'=4,'yl'=2,'core'=2] {'zh'}, dimensions={0}, use_global_device_ids=true | all-gather | bytes 983040 | tf_op jit(solution)/shard_map/all_gather | solution.py:214
  64.1 0.1 dynamic-slice_bitcast_fusion
  64.1 0.1 copy.11.own_ref
  64.2 0.0 all-to-all-done.1
  64.3 0.1 reshape.35.codes_ref
  64.3 14.4 %shard_map.55 = bf16[16,48,512]{2,1,0:T(8,128)(2,1)S(1)} custom-call(s32[1]{0:T(128)} %bitcast.group_ref, s32[96]{0:T(128)S(1)} %reshape.33.start_ref, bf16[4,8,24,512]{3,2,1,0:T(8,128)(2,1)S(1)} %bitcast.8, f32[24,128]{1,0:T(8,128)S(1)} %reshape.35.codes_ref, f32[24,1]{1,0:T(8,128)S(1)} %copy.11.own_ref), custom_call_target="tpu_custom_call" | custom-call | flops 14000000000 | bytes 2097152 | tf_op jit(solution)/shard_map/pallas_call | solution.py:220
  78.7 19.3 %all_to_all.21 = bf16[16,48,512]{2,1,0:T(8,128)(2,1)S(1)} all-to-all(bf16[16,48,512]{2,1,0:T(8,128)(2,1)S(1)} %shard_map.55), channel_id=1, replica_groups=mesh['zh'=4,'zl'=4,'yh'=2,'x'=4,'yl'=2,'core'=2] {'x','yl','core'}, dimensions={0} | all-to-all | bytes 1572864 | tf_op jit(solution)/shard_map/all_to_all | solution.py:242
  98.0 0.1 convert_reduce_fusion
  98.2 12.7 %all_to_all.22 = f32[8,6,512]{2,1,0:T(8,128)S(1)} all-to-all(f32[8,6,512]{2,1,0:T(8,128)S(1)} %reshape.36), channel_id=1, replica_groups=mesh['zh'=4,'zl'=4,'yh'=2,'x'=4,'yl'=2,'core'=2] {'zl','yh'}, dimensions={0} | all-to-all | bytes 196608 | tf_op jit(solution)/shard_map/all_to_all | solution.py:244
  110.9 0.6 mul.40
  (6 shorter events, 0.1 us)
Async XLA Ops:
  0.0 10.8 %copy-start.2 = (s32[96]{0:T(128)S(1)}, s32[96]{0:T(128)}, u32[]{:S(2)}) copy-start(s32[96]{0:T(128)} %param.7) | copy-start | bytes 1156
  0.0 10.8 %copy-start.3 = (s32[96,1]{0,1:T(1,128)S(1)}, s32[96,1]{0,1:T(1,128)}, u32[]{:S(2)}) copy-start(s32[96,1]{0,1:T(1,128)} %param.6) | copy-start | bytes 1156
  0.0 11.2 %copy-start = (s32[192]{0:T(256)S(1)}, s32[192]{0:T(256)}, u32[]{:S(2)}) copy-start(s32[192]{0:T(256)} %param.9) | copy-start | bytes 2308
  0.0 11.2 %copy-start.1 = (s32[192]{0:T(256)S(1)}, s32[192]{0:T(256)}, u32[]{:S(2)}) copy-start(s32[192]{0:T(256)} %param.8) | copy-start | bytes 2308
  1.8 17.2 %all-to-all-start = ((bf16[8,24,512]{2,1,0:T(8,128)(2,1)}), bf16[8,24,512]{2,1,0:T(8,128)(2,1)S(1)}, u32[]{:S(2)}, u32[]{:S(2)}) async-start(bf16[8,24,512]{2,1,0:T(8,128)(2,1)} %bitcast.3), calls=%async_computation | async-start | bytes 393216 | tf_op jit(solution)/shard_map/all_to_all | solution.py:208
  19.6 44.6 %all-to-all-start.1 = ((f32[16,1,192]{2,1,0:T(1,128)}), f32[16,1,192]{2,1,0:T(1,128)S(1)}, u32[]{:S(2)}, u32[]{:S(2)}) async-start(f32[16,1,192]{2,1,0:T(1,128)} %broadcast_in_dim.4), calls=%async_computation.1 | async-start | bytes 32768 | tf_op jit(solution)/shard_map/all_to_all | solution.py:210

commit v4 on v3

--- a/solution.py
+++ b/solution.py
@@ -61,7 +61,7 @@
     return 1.0 / jnp.sqrt(jnp.maximum(square - mean * mean, 0.0) + EPSILON)
 
 
-def shifted_base(tile, n_tiles, base32, base16, place):
+def shifted_base(tile, n_tiles, base32, base16, place, beside):
     chans = tile(0).shape[0]
     lane = lax.broadcasted_iota(jnp.int32, (chans, LANES), 1)
     low = [shift_left(tile(0), i) for i in range(BASE)]
@@ -74,6 +74,7 @@
             base32[pl.ds(i, chans, stride=BASE), :] = jnp.where(lane < LANES - i, low[i], high[i])
         base16[place + q] = base32[...].astype(BF16)
         low = high
+        beside(place + q)
 
 
 def fill_windows(base16, first, count, factor, store):
@@ -123,7 +124,6 @@
         first = (h * n_gather + group_ref[0]) * (RUN * PER_BLOCK)
         values = tiles[pl.ds(first, run_tiles)]
         scale[h * run_tiles : (h + 1) * run_tiles - 1] = weight[None] * deviations(values)
-        shifted_base(lambda q: tiles[first + q], run_tiles, base32, base16, h * run_tiles)
 
     def take_template(row, carry):
         start = start_ref[row]
@@ -141,13 +141,21 @@
     lane = lax.broadcasted_iota(jnp.int32, (NTPL, LANES), 1)
     inside = lane < WIN
     ones = jnp.ones((LANES, LANES), BF16)
-    for c in range(chans):
+    def normalize(c):
+        if c >= chans:
+            return
         values = jnp.where(inside, raw[c * NTPL : (c + 1) * NTPL, :], 0.0)
         mean = dot(values, ones) / WIN
         centred = jnp.where(inside, values - mean, 0.0)
         total = sum(dot(part, ones) for part in two_parts(centred * centred))
         spread = jnp.sqrt(total / WIN + EPSILON)
         tmat[:, c * LANES : (c + 1) * LANES] = (centred / (WIN * spread)).astype(BF16)
+
+    for h in range(n_runs):
+        first = (h * n_gather + group_ref[0]) * (RUN * PER_BLOCK)
+        shifted_base(
+            lambda q: tiles[first + q], run_tiles, base32, base16, h * run_tiles, normalize
+        )
 
     spare = jnp.zeros((LANES - GROUPS * BASE, BLOCK), BF16)
     for win in (win0, win1):
@@ -175,14 +183,14 @@
 
     fill(0, win0)
 
-    def two_blocks(i, carry):
+    def two_blocks(i):
         multiply(2 * i, win0)
         fill(2 * i + 1, win1)
         multiply(2 * i + 1, win1)
         fill(2 * i + 2, win0)
-        return carry
-
-    lax.fori_loop(0, n_split // 2 - 1, two_blocks, 0)
+
+    for i in range(n_split // 2 - 1):
+        two_blocks(i)
     multiply(n_split - 2, win0)
     fill(n_split - 1, win1)
     multiply(n_split - 1, win1)

time: 112 us -> 111 us (level)
  no operation moved by 1% of the time
where the time goes in v4:
time: 111 us
  blocking collectives  69.8 us (63%)
  starting transfers between devices  15.8 us (14%)
  Pallas kernels  13.8 us (12%)
  waiting for transfers between devices  7.82 us (7%)
  other arithmetic  1.92 us (2%)
  local copies, waits for them, and re-layouts  1.77 us (2%)
    all_gather x1, blocking collectives, body(): whole = lax.all_gather(mine, GATHER, axis=0, tiled=False)  37.8 us
    all_to_all x1, blocking collectives, body(): moved = lax.all_to_all(part, STA, 0, 0, tiled=True)  19.3 us
    pallas_call x1, Pallas kernels, body(): pl.pallas_call(stack_kernel, out_shape=jax.ShapeDtypeStruct((n_sta, n_spl...  13.8 us
    all_to_all x1, blocking collectives, body(): final = lax.all_to_all(summed, SPLIT, 0, 0, tiled=True)  12.7 us
    all_to_all x1, starting transfers between devices, body(): mine = lax.all_to_all(rounded, SPLIT, 0, 0, tiled=True)  9.08 us
    all_to_all x1, waiting for transfers between devices, body(): mine = lax.all_to_all(rounded, SPLIT, 0, 0, tiled=True)  7.82 us
    all_to_all x1, starting transfers between devices, body(): lax.all_to_all(jnp.broadcast_to(code[None, :], (n_sta, ch_dev)), STA, 0,...  6.67 us
  transfers between devices with their start and end apart: 2, of which 1 were waited for; matrix products, arithmetic and copies ran while one was open for 0% of the time, Pallas kernels for 0%

profile of v4, /device:TPU:1, one launch (start us, length us, event | category | flops | bytes accessed | tf_op | source)
XLA Modules:
  0.0 110.9 jit_solution(1553529064334545394)
XLA Ops:
  0.0 0.0 copy-start.2
  0.0 0.0 copy-start.3
  0.0 0.0 copy-start
  0.0 0.0 copy-start.1
  0.0 1.7 %convert_element_type.9 = bf16[192,512]{1,0:T(8,128)(2,1)} convert(f32[192,512]{1,0:T(8,128)} %param.5) | non-fusion elementwise | flops 98304 | bytes 589824 | tf_op jit(solution)/shard_map/convert_element_type | solution.py:215
  1.8 9.1 %all-to-all-start = ((bf16[8,24,512]{2,1,0:T(8,128)(2,1)}), bf16[8,24,512]{2,1,0:T(8,128)(2,1)S(1)}, u32[]{:S(2)}, u32[]{:S(2)}) async-start(bf16[8,24,512]{2,1,0:T(8,128)(2,1)} %bitcast.3), calls=%async_computation | async-start | bytes 393216 | tf_op jit(solution)/shard_map/all_to_all | solution.py:216
  10.8 0.0 copy-done.2
  10.8 0.0 copy-done.3
  10.9 0.1 reshape.32
  11.0 0.1 copy.10
  11.1 0.1 reshape.33.start_ref
  11.2 0.0 copy-done
  11.2 0.0 copy-done.1
  11.2 7.8 %all-to-all-done = bf16[8,24,512]{2,1,0:T(8,128)(2,1)S(1)} async-done(((bf16[8,24,512]{2,1,0:T(8,128)(2,1)}), bf16[8,24,512]{2,1,0:T(8,128)(2,1)S(1)}, u32[]{:S(2)}, u32[]{:S(2)}) %all-to-all-start) | async-done | bytes 196640 | tf_op jit(solution)/shard_map/all_to_all | solution.py:216
  19.0 0.6 broadcast_in_dim.4
  19.6 6.7 %all-to-all-start.1 = ((f32[16,1,192]{2,1,0:T(1,128)}), f32[16,1,192]{2,1,0:T(1,128)S(1)}, u32[]{:S(2)}, u32[]{:S(2)}) async-start(f32[16,1,192]{2,1,0:T(1,128)} %broadcast_in_dim.4), calls=%async_computation.1 | async-start | bytes 32768 | tf_op jit(solution)/shard_map/all_to_all | solution.py:218
  26.3 37.8 %all-gather = bf16[32,24,512]{2,1,0:T(8,128)(2,1)S(1)} all-gather(bf16[8,24,512]{2,1,0:T(8,128)(2,1)S(1)} %all-to-all-done), channel_id=2, replica_groups=mesh['zh'=4,'zl'=4,'yh'=2,'x'=4,'yl'=2,'core'=2] {'zh'}, dimensions={0}, use_global_device_ids=true | all-gather | bytes 983040 | tf_op jit(solution)/shard_map/all_gather | solution.py:222
  64.1 0.1 dynamic-slice_bitcast_fusion
  64.1 0.1 copy.11.own_ref
  64.2 0.0 all-to-all-done.1
  64.3 0.1 reshape.35.codes_ref
  64.3 13.8 %shard_map.55 = bf16[16,48,512]{2,1,0:T(8,128)(2,1)S(1)} custom-call(s32[1]{0:T(128)} %bitcast.group_ref, s32[96]{0:T(128)S(1)} %reshape.33.start_ref, bf16[4,8,24,512]{3,2,1,0:T(8,128)(2,1)S(1)} %bitcast.8, f32[24,128]{1,0:T(8,128)S(1)} %reshape.35.codes_ref, f32[24,1]{1,0:T(8,128)S(1)} %copy.11.own_ref), custom_call_target="tpu_custom_call" | custom-call | flops 14000000000 | bytes 2097152 | tf_op jit(solution)/shard_map/pallas_call | solution.py:228
  78.1 19.3 %all_to_all.21 = bf16[16,48,512]{2,1,0:T(8,128)(2,1)S(1)} all-to-all(bf16[16,48,512]{2,1,0:T(8,128)(2,1)S(1)} %shard_map.55), channel_id=1, replica_groups=mesh['zh'=4,'zl'=4,'yh'=2,'x'=4,'yl'=2,'core'=2] {'x','yl','core'}, dimensions={0} | all-to-all | bytes 1572864 | tf_op jit(solution)/shard_map/all_to_all | solution.py:250
  97.4 0.1 convert_reduce_fusion
  97.6 12.7 %all_to_all.22 = f32[8,6,512]{2,1,0:T(8,128)S(1)} all-to-all(f32[8,6,512]{2,1,0:T(8,128)S(1)} %reshape.36), channel_id=1, replica_groups=mesh['zh'=4,'zl'=4,'yh'=2,'x'=4,'yl'=2,'core'=2] {'zl','yh'}, dimensions={0} | all-to-all | bytes 196608 | tf_op jit(solution)/shard_map/all_to_all | solution.py:252
  110.3 0.6 mul.40
  (6 shorter events, 0.1 us)
Async XLA Ops:
  0.0 10.8 %copy-start.2 = (s32[96]{0:T(128)S(1)}, s32[96]{0:T(128)}, u32[]{:S(2)}) copy-start(s32[96]{0:T(128)} %param.7) | copy-start | bytes 1156
  0.0 10.8 %copy-start.3 = (s32[96,1]{0,1:T(1,128)S(1)}, s32[96,1]{0,1:T(1,128)}, u32[]{:S(2)}) copy-start(s32[96,1]{0,1:T(1,128)} %param.6) | copy-start | bytes 1156
  0.0 11.2 %copy-start = (s32[192]{0:T(256)S(1)}, s32[192]{0:T(256)}, u32[]{:S(2)}) copy-start(s32[192]{0:T(256)} %param.9) | copy-start | bytes 2308
  0.0 11.2 %copy-start.1 = (s32[192]{0:T(256)S(1)}, s32[192]{0:T(256)}, u32[]{:S(2)}) copy-start(s32[192]{0:T(256)} %param.8) | copy-start | bytes 2308
  1.8 17.2 %all-to-all-start = ((bf16[8,24,512]{2,1,0:T(8,128)(2,1)}), bf16[8,24,512]{2,1,0:T(8,128)(2,1)S(1)}, u32[]{:S(2)}, u32[]{:S(2)}) async-start(bf16[8,24,512]{2,1,0:T(8,128)(2,1)} %bitcast.3), calls=%async_computation | async-start | bytes 393216 | tf_op jit(solution)/shard_map/all_to_all | solution.py:216
  19.6 44.6 %all-to-all-start.1 = ((f32[16,1,192]{2,1,0:T(1,128)}), f32[16,1,192]{2,1,0:T(1,128)S(1)}, u32[]{:S(2)}, u32[]{:S(2)}) async-start(f32[16,1,192]{2,1,0:T(1,128)} %broadcast_in_dim.4), calls=%async_computation.1 | async-start | bytes 32768 | tf_op jit(solution)/shard_map/all_to_all | solution.py:218

commit v5 on v3

--- a/solution.py
+++ b/solution.py
@@ -22,6 +22,8 @@
 SPLIT = ("zl", "yh")
 GATHER = "zh"
 STA = ("x", "yl", "core")
+CHIPS = ("x", "yl")
+CORES = 2
 
 SMEM = pl.BlockSpec(memory_space=pltpu.SMEM)
 VMEM = pl.BlockSpec(memory_space=pltpu.VMEM)
@@ -188,8 +190,9 @@
     multiply(n_split - 1, win1)
     rows = n_split * per_sta
     for j in range(n_sta):
+        place = j % CORES * (n_sta // CORES) + j // CORES
         for q in range(PER_BLOCK):
-            out_ref[j, :, q * LANES : (q + 1) * LANES] = acc[
+            out_ref[place, :, q * LANES : (q + 1) * LANES] = acc[
                 q, j * rows : (j + 1) * rows, :
             ].astype(BF16)
 
@@ -239,7 +242,10 @@
         ),
     )(group, starts, whole, codes, own)
 
-    moved = lax.all_to_all(part, STA, 0, 0, tiled=True)
+    pair = lax.all_to_all(part, "core", 0, 0, tiled=True)
+    pair = pair.reshape(CORES, n_sta // CORES, n_split * per_sta, samp_dev)
+    half = jnp.sum(pair.astype(F32), axis=0).astype(BF16)
+    moved = lax.all_to_all(half, CHIPS, 0, 0, tiled=True)
     summed = jnp.sum(moved.astype(F32), axis=0).reshape(n_split, per_sta, samp_dev)
     final = lax.all_to_all(summed, SPLIT, 0, 0, tiled=True)
     result = jnp.sum(final, axis=0) * (1.0 / 32.0)

time: 112 us -> 111 us (level)
  blocking collectives: 69.7 us -> 68 us
  local copies, waits for them, and re-layouts: 1.77 us -> 3.11 us
  waiting for transfers between devices: 7.82 us -> 6.48 us
    all_to_all x1 -> x2, blocking collectives: 19.3 us -> 17.6 us  [the longest x1 12.5 us: body(): moved = lax.all_to_all(half, CHIPS, 0, 0, tiled=True)]
    unnamed x8, local copies, waits for them, and re-layouts: 0.02 us -> 1.36 us
    all_to_all x1, waiting for transfers between devices: 7.82 us -> 6.48 us  [body(): mine = lax.all_to_all(rounded, SPLIT, 0, 0, tiled=True)]
where the time goes in v5:
time: 111 us; the launch traced here: 110 us
  blocking collectives  68 us (61%)
  starting transfers between devices  15.8 us (14%)
  Pallas kernels  14.4 us (13%)
  waiting for transfers between devices  6.48 us (6%)
  local copies, waits for them, and re-layouts  3.11 us (3%)
  other arithmetic  1.97 us (2%)
    all_gather x1, blocking collectives, body(): whole = lax.all_gather(mine, GATHER, axis=0, tiled=False)  37.8 us
    pallas_call x1, Pallas kernels, body(): pl.pallas_call(stack_kernel, out_shape=jax.ShapeDtypeStruct((n_sta, n_spl...  14.4 us
    all_to_all x1, blocking collectives, body(): final = lax.all_to_all(summed, SPLIT, 0, 0, tiled=True)  12.6 us
    all_to_all x1, blocking collectives, body(): moved = lax.all_to_all(half, CHIPS, 0, 0, tiled=True)  12.5 us
    all_to_all x1, starting transfers between devices, body(): mine = lax.all_to_all(rounded, SPLIT, 0, 0, tiled=True)  9.08 us
    all_to_all x1, starting transfers between devices, body(): lax.all_to_all(jnp.broadcast_to(code[None, :], (n_sta, ch_dev)), STA, 0,...  6.67 us
    all_to_all x1, waiting for transfers between devices, body(): mine = lax.all_to_all(rounded, SPLIT, 0, 0, tiled=True)  6.48 us
    all_to_all x1, blocking collectives, body(): pair = lax.all_to_all(part, 'core', 0, 0, tiled=True)  5.07 us
  transfers between devices with their start and end apart: 2, of which 1 were waited for; matrix products, arithmetic and copies ran while one was open for 0% of the time, Pallas kernels for 0%

profile of v5, /device:TPU:1, one launch (start us, length us, event | category | flops | bytes accessed | tf_op | source)
XLA Modules:
  0.0 109.8 jit_solution(8317782026588063949)
XLA Ops:
  0.0 1.7 %convert_element_type.11 = bf16[192,512]{1,0:T(8,128)(2,1)} convert(f32[192,512]{1,0:T(8,128)} %param.5) | non-fusion elementwise | flops 98304 | bytes 589824 | tf_op jit(solution)/shard_map/convert_element_type | solution.py:210
  1.7 9.1 %all-to-all-start = ((bf16[8,24,512]{2,1,0:T(8,128)(2,1)}), bf16[8,24,512]{2,1,0:T(8,128)(2,1)S(1)}, u32[]{:S(2)}, u32[]{:S(2)}) async-start(bf16[8,24,512]{2,1,0:T(8,128)(2,1)} %bitcast.3), calls=%async_computation | async-start | bytes 393216 | tf_op jit(solution)/shard_map/all_to_all | solution.py:211
  10.8 0.0 copy-start.2
  10.8 0.0 copy-start.3
  10.8 0.6 copy-done.2
  11.4 0.0 copy-done.3
  11.4 0.1 reshape.35
  11.6 0.1 copy.12
  11.7 0.1 reshape.36.start_ref
  11.7 0.0 copy-start
  11.7 0.0 copy-start.1
  11.8 0.7 copy-done
  12.4 0.0 copy-done.1
  12.5 6.5 %all-to-all-done = bf16[8,24,512]{2,1,0:T(8,128)(2,1)S(1)} async-done(((bf16[8,24,512]{2,1,0:T(8,128)(2,1)}), bf16[8,24,512]{2,1,0:T(8,128)(2,1)S(1)}, u32[]{:S(2)}, u32[]{:S(2)}) %all-to-all-start) | async-done | bytes 196640 | tf_op jit(solution)/shard_map/all_to_all | solution.py:211
  18.9 0.6 broadcast_in_dim.4
  19.5 6.7 %all-to-all-start.1 = ((f32[16,1,192]{2,1,0:T(1,128)}), f32[16,1,192]{2,1,0:T(1,128)S(1)}, u32[]{:S(2)}, u32[]{:S(2)}) async-start(f32[16,1,192]{2,1,0:T(1,128)} %broadcast_in_dim.4), calls=%async_computation.1 | async-start | bytes 32768 | tf_op jit(solution)/shard_map/all_to_all | solution.py:213
  26.2 37.8 %all-gather = bf16[32,24,512]{2,1,0:T(8,128)(2,1)S(1)} all-gather(bf16[8,24,512]{2,1,0:T(8,128)(2,1)S(1)} %all-to-all-done), channel_id=2, replica_groups=mesh['zh'=4,'zl'=4,'yh'=2,'x'=4,'yl'=2,'core'=2] {'zh'}, dimensions={0}, use_global_device_ids=true | all-gather | bytes 983040 | tf_op jit(solution)/shard_map/all_gather | solution.py:217
  64.0 0.1 dynamic-slice_bitcast_fusion
  64.1 0.1 copy.13.own_ref
  64.2 0.0 all-to-all-done.1
  64.2 0.1 reshape.38.codes_ref
  64.3 14.4 %shard_map.55 = bf16[16,48,512]{2,1,0:T(8,128)(2,1)S(1)} custom-call(s32[1]{0:T(128)} %bitcast.group_ref, s32[96]{0:T(128)S(1)} %reshape.36.start_ref, bf16[4,8,24,512]{3,2,1,0:T(8,128)(2,1)S(1)} %bitcast.9, f32[24,128]{1,0:T(8,128)S(1)} %reshape.38.codes_ref, f32[24,1]{1,0:T(8,128)S(1)} %copy.13.own_ref), custom_call_target="tpu_custom_call" | custom-call | flops 14000000000 | bytes 2097152 | tf_op jit(solution)/shard_map/pallas_call | solution.py:223
  78.7 5.1 %all_to_all.26 = bf16[16,48,512]{2,1,0:T(8,128)(2,1)S(1)} all-to-all(bf16[16,48,512]{2,1,0:T(8,128)(2,1)S(1)} %shard_map.55), channel_id=1, replica_groups=mesh['zh'=4,'zl'=4,'yh'=2,'x'=4,'yl'=2,'core'=2] {'core'}, dimensions={0} | all-to-all | bytes 1572864 | tf_op jit(solution)/shard_map/all_to_all | solution.py:245
  83.7 0.2 reduce_sum.30
  83.9 12.5 %all_to_all.27 = bf16[8,48,512]{2,1,0:T(8,128)(2,1)S(1)} all-to-all(bf16[8,48,512]{2,1,0:T(8,128)(2,1)S(1)} %reduce_sum.30), channel_id=1, replica_groups=mesh['zh'=4,'zl'=4,'yh'=2,'x'=4,'yl'=2,'core'=2] {'x','yl'}, dimensions={0} | all-to-all | bytes 786432 | tf_op jit(solution)/shard_map/all_to_all | solution.py:248
  96.4 0.1 convert_reduce_fusion
  96.5 12.6 %all_to_all.28 = f32[8,6,512]{2,1,0:T(8,128)S(1)} all-to-all(f32[8,6,512]{2,1,0:T(8,128)S(1)} %reshape.40), channel_id=1, replica_groups=mesh['zh'=4,'zl'=4,'yh'=2,'x'=4,'yl'=2,'core'=2] {'zl','yh'}, dimensions={0} | all-to-all | bytes 196608 | tf_op jit(solution)/shard_map/all_to_all | solution.py:250
  109.1 0.6 mul.40
  (6 shorter events, 0.1 us)
Async XLA Ops:
  1.7 17.2 %all-to-all-start = ((bf16[8,24,512]{2,1,0:T(8,128)(2,1)}), bf16[8,24,512]{2,1,0:T(8,128)(2,1)S(1)}, u32[]{:S(2)}, u32[]{:S(2)}) async-start(bf16[8,24,512]{2,1,0:T(8,128)(2,1)} %bitcast.3), calls=%async_computation | async-start | bytes 393216 | tf_op jit(solution)/shard_map/all_to_all | solution.py:211
  10.8 0.7 copy-start.2
  10.8 0.7 copy-start.3
  11.7 0.7 copy-start
  11.7 0.7 copy-start.1
  19.5 44.6 %all-to-all-start.1 = ((f32[16,1,192]{2,1,0:T(1,128)}), f32[16,1,192]{2,1,0:T(1,128)S(1)}, u32[]{:S(2)}, u32[]{:S(2)}) async-start(f32[16,1,192]{2,1,0:T(1,128)} %broadcast_in_dim.4), calls=%async_computation.1 | async-start | bytes 32768 | tf_op jit(solution)/shard_map/all_to_all | solution.py:213

commit v6 on v3

--- a/solution.py
+++ b/solution.py
@@ -241,8 +241,8 @@
 
     moved = lax.all_to_all(part, STA, 0, 0, tiled=True)
     summed = jnp.sum(moved.astype(F32), axis=0).reshape(n_split, per_sta, samp_dev)
-    final = lax.all_to_all(summed, SPLIT, 0, 0, tiled=True)
-    result = jnp.sum(final, axis=0) * (1.0 / 32.0)
+    final = lax.all_to_all(summed.astype(BF16), SPLIT, 0, 0, tiled=True)
+    result = jnp.sum(final.astype(F32), axis=0) * (1.0 / 32.0)
     return result.reshape(NSTEP, per_sta // NSTEP, samp_dev)
 
 

time: 112 us -> 111 us (level)
  local copies, waits for them, and re-layouts: 1.77 us -> 3.12 us
  waiting for transfers between devices: 7.82 us -> 6.48 us
    unnamed x8, local copies, waits for them, and re-layouts: 0.02 us -> 1.36 us
    all_to_all x1, waiting for transfers between devices: 7.82 us -> 6.48 us  [body(): mine = lax.all_to_all(rounded, SPLIT, 0, 0, tiled=True)]
where the time goes in v6:
time: 111 us
  blocking collectives  69.3 us (62%)
  starting transfers between devices  15.8 us (14%)
  Pallas kernels  14.4 us (13%)
  waiting for transfers between devices  6.48 us (6%)
  local copies, waits for them, and re-layouts  3.12 us (3%)
  other arithmetic  1.88 us (2%)
    all_gather x1, blocking collectives, body(): whole = lax.all_gather(mine, GATHER, axis=0, tiled=False)  37.8 us
    all_to_all x1, blocking collectives, body(): moved = lax.all_to_all(part, STA, 0, 0, tiled=True)  19.3 us
    pallas_call x1, Pallas kernels, body(): pl.pallas_call(stack_kernel, out_shape=jax.ShapeDtypeStruct((n_sta, n_spl...  14.4 us
    all_to_all x1, blocking collectives, body(): final = lax.all_to_all(summed.astype(BF16), SPLIT, 0, 0, tiled=True)  12.2 us
    all_to_all x1, starting transfers between devices, body(): mine = lax.all_to_all(rounded, SPLIT, 0, 0, tiled=True)  9.08 us
    all_to_all x1, starting transfers between devices, body(): lax.all_to_all(jnp.broadcast_to(code[None, :], (n_sta, ch_dev)), STA, 0,...  6.67 us
    all_to_all x1, waiting for transfers between devices, body(): mine = lax.all_to_all(rounded, SPLIT, 0, 0, tiled=True)  6.48 us
  transfers between devices with their start and end apart: 2, of which 1 were waited for; matrix products, arithmetic and copies ran while one was open for 0% of the time, Pallas kernels for 0%

profile of v6, /device:TPU:1, one launch (start us, length us, event | category | flops | bytes accessed | tf_op | source)
XLA Modules:
  0.0 110.9 jit_solution(12486132279649307321)
XLA Ops:
  0.0 1.7 %convert_element_type.14 = bf16[192,512]{1,0:T(8,128)(2,1)} convert(f32[192,512]{1,0:T(8,128)} %param.5) | non-fusion elementwise | flops 98304 | bytes 589824 | tf_op jit(solution)/shard_map/convert_element_type | solution.py:207
  1.7 9.1 %all-to-all-start = ((bf16[8,24,512]{2,1,0:T(8,128)(2,1)}), bf16[8,24,512]{2,1,0:T(8,128)(2,1)S(1)}, u32[]{:S(2)}, u32[]{:S(2)}) async-start(bf16[8,24,512]{2,1,0:T(8,128)(2,1)} %bitcast.3), calls=%async_computation | async-start | bytes 393216 | tf_op jit(solution)/shard_map/all_to_all | solution.py:208
  10.8 0.0 copy-start.2
  10.8 0.0 copy-start.3
  10.8 0.6 copy-done.2
  11.4 0.0 copy-done.3
  11.4 0.1 reshape.31
  11.6 0.1 copy.10
  11.7 0.1 reshape.32.start_ref
  11.7 0.0 copy-start
  11.7 0.0 copy-start.1
  11.8 0.7 copy-done
  12.4 0.0 copy-done.1
  12.5 6.5 %all-to-all-done = bf16[8,24,512]{2,1,0:T(8,128)(2,1)S(1)} async-done(((bf16[8,24,512]{2,1,0:T(8,128)(2,1)}), bf16[8,24,512]{2,1,0:T(8,128)(2,1)S(1)}, u32[]{:S(2)}, u32[]{:S(2)}) %all-to-all-start) | async-done | bytes 196640 | tf_op jit(solution)/shard_map/all_to_all | solution.py:208
  18.9 0.6 broadcast_in_dim.4
  19.5 6.7 %all-to-all-start.1 = ((f32[16,1,192]{2,1,0:T(1,128)}), f32[16,1,192]{2,1,0:T(1,128)S(1)}, u32[]{:S(2)}, u32[]{:S(2)}) async-start(f32[16,1,192]{2,1,0:T(1,128)} %broadcast_in_dim.4), calls=%async_computation.1 | async-start | bytes 32768 | tf_op jit(solution)/shard_map/all_to_all | solution.py:210
  26.2 37.8 %all-gather = bf16[32,24,512]{2,1,0:T(8,128)(2,1)S(1)} all-gather(bf16[8,24,512]{2,1,0:T(8,128)(2,1)S(1)} %all-to-all-done), channel_id=2, replica_groups=mesh['zh'=4,'zl'=4,'yh'=2,'x'=4,'yl'=2,'core'=2] {'zh'}, dimensions={0}, use_global_device_ids=true | all-gather | bytes 983040 | tf_op jit(solution)/shard_map/all_gather | solution.py:214
  64.0 0.1 dynamic-slice_bitcast_fusion
  64.1 0.1 copy.11.own_ref
  64.2 0.0 all-to-all-done.1
  64.2 0.1 reshape.34.codes_ref
  64.3 14.4 %shard_map.55 = bf16[16,48,512]{2,1,0:T(8,128)(2,1)S(1)} custom-call(s32[1]{0:T(128)} %bitcast.group_ref, s32[96]{0:T(128)S(1)} %reshape.32.start_ref, bf16[4,8,24,512]{3,2,1,0:T(8,128)(2,1)S(1)} %bitcast.8, f32[24,128]{1,0:T(8,128)S(1)} %reshape.34.codes_ref, f32[24,1]{1,0:T(8,128)S(1)} %copy.11.own_ref), custom_call_target="tpu_custom_call" | custom-call | flops 14000000000 | bytes 2097152 | tf_op jit(solution)/shard_map/pallas_call | solution.py:220
  78.7 19.3 %all_to_all.21 = bf16[16,48,512]{2,1,0:T(8,128)(2,1)S(1)} all-to-all(bf16[16,48,512]{2,1,0:T(8,128)(2,1)S(1)} %shard_map.55), channel_id=1, replica_groups=mesh['zh'=4,'zl'=4,'yh'=2,'x'=4,'yl'=2,'core'=2] {'x','yl','core'}, dimensions={0} | all-to-all | bytes 1572864 | tf_op jit(solution)/shard_map/all_to_all | solution.py:242
  98.0 0.1 reduce_sum.21
  98.1 12.2 %all_to_all.22 = bf16[8,6,512]{2,1,0:T(8,128)(2,1)S(1)} all-to-all(bf16[8,6,512]{2,1,0:T(8,128)(2,1)S(1)} %convert_element_type.16), channel_id=1, replica_groups=mesh['zh'=4,'zl'=4,'yh'=2,'x'=4,'yl'=2,'core'=2] {'zl','yh'}, dimensions={0} | all-to-all | bytes 98304 | tf_op jit(solution)/shard_map/all_to_all | solution.py:244
  110.3 0.6 mul.40
  (6 shorter events, 0.1 us)
Async XLA Ops:
  1.7 17.2 %all-to-all-start = ((bf16[8,24,512]{2,1,0:T(8,128)(2,1)}), bf16[8,24,512]{2,1,0:T(8,128)(2,1)S(1)}, u32[]{:S(2)}, u32[]{:S(2)}) async-start(bf16[8,24,512]{2,1,0:T(8,128)(2,1)} %bitcast.3), calls=%async_computation | async-start | bytes 393216 | tf_op jit(solution)/shard_map/all_to_all | solution.py:208
  10.8 0.7 copy-start.2
  10.8 0.7 copy-start.3
  11.7 0.7 copy-start
  11.7 0.7 copy-start.1
  19.5 44.6 %all-to-all-start.1 = ((f32[16,1,192]{2,1,0:T(1,128)}), f32[16,1,192]{2,1,0:T(1,128)S(1)}, u32[]{:S(2)}, u32[]{:S(2)}) async-start(f32[16,1,192]{2,1,0:T(1,128)} %broadcast_in_dim.4), calls=%async_computation.1 | async-start | bytes 32768 | tf_op jit(solution)/shard_map/all_to_all | solution.py:210
